TPU v7x, 512 devices: a whole 4x4x16 slice. The times are simulated.
512 devices in a mesh: seq: 4 (over y), exp: 128 (over z, x, core).
Axes of the slice: x: 4, y: 4, z: 16, core: 2. Of those that a mesh axis runs over, the one named last changes fastest.
Arguments:
- out_grad: bfloat16 [65536, 4096], P(('seq', 'exp')), may hold values from -2 to 2
- expert_ids: int32 [65536, 2], P(('seq', 'exp')), may hold values from 0 to 127, all different within a row; in each aligned block of 128 rows (0 to 127, 128 to 255, ...) at most 3 rows name the same one
- route_weights: bfloat16 [65536, 2], P(('seq', 'exp')), may hold values from 0.099609375 to 1
- down_weight: bfloat16 [128, 768, 4096], P('exp', 'seq'), may hold values from -0.21875 to 0.21875
- gate_pre: bfloat16 [128, 1536, 768], P('exp', None, 'seq'), may hold values from -6 to 6
- up_pre: bfloat16 [128, 1536, 768], P('exp', None, 'seq'), may hold values from -6 to 6
Outputs:
- grad_gate: bfloat16 [128, 1536, 768], P('exp', None, 'seq')
- grad_up: bfloat16 [128, 1536, 768], P('exp', None, 'seq')
- route_grad: float32 [65536, 2], P(('seq', 'exp'))
Inputs may be any that keep to these rules, and one draw needn't show every extreme that they name: `expert_ids`: A token's 2 slots name different experts. Among the slots of one device no expert is named more than 3 times, and in every draw some expert is named exactly 3 times by some device.
All inputs are finite; a program needn't handle non-finite values.
Results may differ from a plain program's by a relative error of at most 0.001.
Values may be sent and summed in bfloat16 or wider, within the bound.
A program may use at most 64 MiB of HBM per device.

v0:
```python
import jax
import jax.numpy as jnp
from jax import lax
from jax.sharding import PartitionSpec as P


def expert_backward(slot_rows, slot_weights, down_rows, gate_saved, up_saved):
    projected = lax.dot_general(
        slot_rows, down_rows, (((1,), (1,)), ((), ())), preferred_element_type=jnp.float32
    )
    gate_value = gate_saved.astype(jnp.float32)
    up_value = up_saved.astype(jnp.float32)
    sigmoid_gate = jax.nn.sigmoid(gate_value)
    activated = gate_value * sigmoid_gate
    partial_value = jnp.sum(activated * up_value * projected, axis=1)
    scaled = slot_weights.astype(jnp.float32)[:, None] * projected
    grad_up = scaled * activated
    grad_gate = scaled * up_value * sigmoid_gate * (1.0 + gate_value * (1.0 - sigmoid_gate))
    return (grad_gate, grad_up, partial_value)


def per_device(out_grad, expert_ids, route_weights, down_weight, gate_pre, up_pre):
    tokens, slot_count = expert_ids.shape
    model_width = out_grad.shape[1]
    experts = lax.axis_size("exp")
    groups = lax.axis_size("seq")
    capacity = gate_pre.shape[1] // (groups * experts)
    flat_ids = expert_ids.reshape(-1)
    onehot = (flat_ids[:, None] == jnp.arange(experts, dtype=jnp.int32)[None, :]).astype(jnp.int32)
    slot_ranks = jnp.sum((jnp.cumsum(onehot, axis=0) - onehot) * onehot, axis=1)
    target = flat_ids * capacity + slot_ranks
    sentinel = tokens * slot_count
    slot_table = jnp.full((experts * capacity,), sentinel, jnp.int32)
    slot_table = slot_table.at[target].set(jnp.arange(sentinel, dtype=jnp.int32))
    padded_rows = jnp.concatenate([out_grad, jnp.zeros((1, model_width), out_grad.dtype)], axis=0)
    padded_weights = jnp.concatenate(
        [route_weights.reshape(-1), jnp.zeros((1,), route_weights.dtype)]
    )
    outgoing = padded_rows[slot_table // slot_count].reshape(experts, capacity, model_width)
    outgoing_weights = padded_weights[slot_table].reshape(experts, capacity)
    arrived, arrived_weights = (
        lax.all_to_all(outgoing, "exp", split_axis=0, concat_axis=0, tiled=True),
        lax.all_to_all(outgoing_weights, "exp", split_axis=0, concat_axis=0, tiled=True),
    )
    local_rows = arrived.reshape(experts * capacity, model_width)
    local_weights = arrived_weights.reshape(-1)
    all_rows, all_weights = (
        lax.all_gather(local_rows, "seq", axis=0, tiled=True),
        lax.all_gather(local_weights, "seq", axis=0, tiled=True),
    )
    grad_gate, grad_up, partial_value = expert_backward(
        all_rows, all_weights, down_weight[0], gate_pre[0], up_pre[0]
    )
    scores = lax.psum_scatter(partial_value, "seq", scatter_dimension=0, tiled=True)
    gate_out = grad_gate.astype(jnp.bfloat16)[None]
    up_out = grad_up.astype(jnp.bfloat16)[None]
    returned = lax.all_to_all(
        scores.reshape(experts, capacity), "exp", split_axis=0, concat_axis=0, tiled=True
    )
    route_grad = returned.reshape(-1)[target].reshape(tokens, slot_count)
    return (gate_out, up_out, route_grad)


def solution(mesh):
    placed = (
        P(("seq", "exp"), None),
        P(("seq", "exp"), None),
        P(("seq", "exp"), None),
        P("exp", "seq", None),
        P("exp", None, "seq"),
        P("exp", None, "seq"),
    )
    return jax.shard_map(
        per_device,
        mesh=mesh,
        in_specs=placed,
        out_specs=(P("exp", None, "seq"), P("exp", None, "seq"), P(("seq", "exp"), None)),
        check_vma=False,
    )
```

profile of v0, /device:TPU:1, one launch (start us, length us, event | category | flops | bytes accessed | tf_op | source)
XLA Modules:
  0.0 423.6 jit_solution(7672190468829769690)
XLA Ops:
  7.2 0.9 copy.18
  8.3 0.1 eq.25
  8.4 0.7 broadcast_multiply_fusion
  9.2 0.2 fusion.13
  9.8 0.2 fusion.15
  10.0 1.4 scatter_custom_fusion
  11.4 1.3 concatenate.7
  12.7 4.1 gather_fusion.1
  16.8 7.1 %reshape.88 = bf16[128,3,4096]{2,1,0:T(4,128)(2,1)} reshape(bf16[384,4096]{1,0:T(8,128)(2,1)} %gather_fusion.1) | data formatting | bytes 6291456 | tf_op jit(solution)/shard_map/reshape | solution.py:39
  23.9 204.4 %all_to_all.24 = bf16[128,3,4096]{2,1,0:T(4,128)(2,1)} all-to-all(bf16[128,3,4096]{2,1,0:T(4,128)(2,1)} %reshape.88), channel_id=1, replica_groups=mesh['seq'=4,'exp'=128] {'exp'}, dimensions={0} | all-to-all | bytes 6291456 | tf_op jit(solution)/shard_map/all_to_all | solution.py:42
  228.2 7.4 %reshape.89 = bf16[384,4096]{1,0:T(8,128)(2,1)} reshape(bf16[128,3,4096]{2,1,0:T(4,128)(2,1)} %all_to_all.24) | data formatting | bytes 6291456 | tf_op jit(solution)/shard_map/reshape | solution.py:45
  235.7 0.6 copy-done.1
  236.5 0.1 reshape.85
  236.6 2.8 gather_fusion
  239.5 0.9 all_to_all.20
  240.4 13.1 %all-to-all-start = ((bf16[128,1,3]{2,1,0:T(2,128)(2,1)}), bf16[128,1,3]{2,1,0:T(2,128)(2,1)S(1)}, u32[]{:S(2)}, u32[]{:S(2)}) async-start(bf16[128,1,3]{2,1,0:T(2,128)(2,1)} %all_to_all.20), calls=%async_computation | async-start | bytes 131072 | tf_op jit(solution)/shard_map/all_to_all | solution.py:43
  253.5 1.3 dynamic-slice
  255.4 12.9 %all-to-all-done = bf16[128,1,3]{2,1,0:T(2,128)(2,1)S(1)} async-done(((bf16[128,1,3]{2,1,0:T(2,128)(2,1)}), bf16[128,1,3]{2,1,0:T(2,128)(2,1)S(1)}, u32[]{:S(2)}, u32[]{:S(2)}) %all-to-all-start) | async-done | bytes 800 | tf_op jit(solution)/shard_map/all_to_all | solution.py:43
  268.3 0.2 reduce
  268.5 0.2 reshape.128
  268.7 9.8 %all-gather = bf16[4,1,384]{2,1,0:T(2,128)(2,1)S(1)} all-gather(bf16[1,1,384]{2,1,0:T(2,128)(2,1)S(1)} %reshape.128), channel_id=1, replica_groups=mesh['seq'=4,'exp'=128] {'seq'}, dimensions={0}, use_global_device_ids=true | all-gather | bytes 3840 | tf_op jit(solution)/shard_map/all_gather | solution.py:49
  278.6 81.6 %all-gather.3.cloned.1.call-done = bf16[1536,4096]{1,0:T(8,128)(2,1)} async-done(((bf16[384,4096]{1,0:T(8,128)(2,1)}), bf16[1536,4096]{1,0:T(8,128)(2,1)}) %all-gather.3.cloned.1.call-update) | async-done | bytes 12582928 | tf_op jit(solution)/shard_map/all_gather | solution.py:48
  360.2 10.4 %fusion.6 = (f32[1536]{0:T(1024)S(1)}, bf16[1,1536,192]{1,2,0:T(8,128)(2,1)}, bf16[1,1536,192]{1,2,0:T(8,128)(2,1)}) fusion(bf16[1,1536,192]{1,2,0:T(8,128)(2,1)S(1)} %copy-done.2, bf16[1,1536,192]{1,2,0:T(8,128)(2,1)S(1)} %copy-done.3, f32[1536]{0:T(1024)S(1)} %reshape.130, bf16[1536,4096]{1,0:T(8,128)(2,1)} %all-gather.3.cloned.1.call-done, ...), kind=kOutput, calls=%fused_computation.15 | convolution fusion | flops 2421520896 | bytes 16527360 | tf_op jit(solution)/shard_map/dot_general | solution.py:8
  370.6 7.3 %all-reduce.1 = f32[1536]{0:T(1024)S(1)} all-reduce(f32[1536]{0:T(1024)S(1)} %get-tuple-element.9), channel_id=2, replica_groups=mesh['seq'=4,'exp'=128] {'seq'}, use_global_device_ids=true, to_apply=%region_5.6.clone | all-reduce | flops 1536 | bytes 12288
  377.9 0.8 all_to_all.18
  378.8 18.9 %all-to-all-start.2 = ((f32[128,1,3]{2,1,0:T(1,128)}), f32[128,1,3]{2,1,0:T(1,128)S(1)}, u32[]{:S(2)}, u32[]{:S(2)}) async-start(f32[128,1,3]{2,1,0:T(1,128)} %bitcast.12), calls=%async_computation.2 | async-start | bytes 131072 | tf_op jit(solution)/shard_map/all_to_all | solution.py:57
  397.7 14.8 %all-to-all-done.2 = f32[128,1,3]{2,1,0:T(1,128)S(1)} async-done(((f32[128,1,3]{2,1,0:T(1,128)}), f32[128,1,3]{2,1,0:T(1,128)S(1)}, u32[]{:S(2)}, u32[]{:S(2)}) %all-to-all-start.2) | async-done | bytes 1568 | tf_op jit(solution)/shard_map/all_to_all | solution.py:57
  412.5 0.5 broadcast.94
  413.0 0.8 reduce.6
  413.8 0.2 reshape.90
  414.0 1.9 gather_fusion.2
  416.1 0.6 copy.24
  (30 shorter events, 1.1 us)
Async XLA Ops:
  7.2 353.0 %copy-start = (bf16[1,192,4096]{2,1,0:T(8,128)(2,1)S(1)}, bf16[1,192,4096]{2,1,0:T(8,128)(2,1)}, u32[]{:S(2)}) copy-start(bf16[1,192,4096]{2,1,0:T(8,128)(2,1)} %param.9) | copy-start | bytes 4718596
  7.2 353.0 %all-gather.3.cloned.1.call-start = ((), (), s32[]{:S(2)}) async-start(), calls=%async_computation.3 | async-start | bytes 15728640 | tf_op jit(solution)/shard_map/all_gather | solution.py:48
  235.7 0.7 copy-start.1
  236.3 123.8 %copy-start.2 = (bf16[1,1536,192]{1,2,0:T(8,128)(2,1)S(1)}, bf16[1,1536,192]{1,2,0:T(8,128)(2,1)}, u32[]{:S(2)}) copy-start(bf16[1,1536,192]{1,2,0:T(8,128)(2,1)} %param.11) | copy-start | bytes 1769476
  236.3 123.8 %copy-start.3 = (bf16[1,1536,192]{1,2,0:T(8,128)(2,1)S(1)}, bf16[1,1536,192]{1,2,0:T(8,128)(2,1)}, u32[]{:S(2)}) copy-start(bf16[1,1536,192]{1,2,0:T(8,128)(2,1)} %param.10) | copy-start | bytes 1769476
  240.4 28.0 %all-to-all-start = ((bf16[128,1,3]{2,1,0:T(2,128)(2,1)}), bf16[128,1,3]{2,1,0:T(2,128)(2,1)S(1)}, u32[]{:S(2)}, u32[]{:S(2)}) async-start(bf16[128,1,3]{2,1,0:T(2,128)(2,1)} %all_to_all.20), calls=%async_computation | async-start | bytes 131072 | tf_op jit(solution)/shard_map/all_to_all | solution.py:43
  378.8 33.7 %all-to-all-start.2 = ((f32[128,1,3]{2,1,0:T(1,128)}), f32[128,1,3]{2,1,0:T(1,128)S(1)}, u32[]{:S(2)}, u32[]{:S(2)}) async-start(f32[128,1,3]{2,1,0:T(1,128)} %bitcast.12), calls=%async_computation.2 | async-start | bytes 131072 | tf_op jit(solution)/shard_map/all_to_all | solution.py:57
Sparse Core Ops, SparseCore 0:
  235.8 124.3 all-gather.2
where the time goes:
time: 424 us
  blocking collectives  221 us (52%)
  waiting for transfers between devices  109 us (26%)
  local copies, waits for them, and re-layouts  33.3 us (8%)
  starting transfers between devices  32.1 us (8%)
  between operations  14.9 us (4%)
  matrix products  10.4 us (2%)
    all_to_all x1, blocking collectives, per_device(): lax.all_to_all(outgoing, 'exp', split_axis=0, concat_axis=0, tiled=True)  204 us
    all_gather x1, waiting for transfers between devices, per_device(): lax.all_gather(local_rows, 'seq', axis=0, tiled=True)  81.6 us
    all_to_all x1, starting transfers between devices, per_device(): lax.all_to_all(scores.reshape(experts, capacity), 'exp', split_axis=0, co...  18.9 us
    all_to_all x1, waiting for transfers between devices, per_device(): lax.all_to_all(scores.reshape(experts, capacity), 'exp', split_axis=0, co...  14.8 us
    all_to_all x1, starting transfers between devices, per_device(): lax.all_to_all(outgoing_weights, 'exp', split_axis=0, concat_axis=0, tile...  13.1 us
    all_to_all x1, waiting for transfers between devices, per_device(): lax.all_to_all(outgoing_weights, 'exp', split_axis=0, concat_axis=0, tile...  12.9 us
    dot_general x1, matrix products, expert_backward(): lax.dot_general(slot_rows, down_rows, (((1,), (1,)), ((), ())), preferred...  10.4 us
    all_gather x1, blocking collectives, per_device(): lax.all_gather(local_weights, 'seq', axis=0, tiled=True)  9.82 us
  transfers between devices with their start and end apart: 3, of which 3 were waited for; matrix products, arithmetic and copies ran while one was open for 1% of the time, Pallas kernels for 0%

commit v1 on v0

--- a/solution.py
+++ b/solution.py
@@ -4,10 +4,7 @@
 from jax.sharding import PartitionSpec as P
 
 
-def expert_backward(slot_rows, slot_weights, down_rows, gate_saved, up_saved):
-    projected = lax.dot_general(
-        slot_rows, down_rows, (((1,), (1,)), ((), ())), preferred_element_type=jnp.float32
-    )
+def expert_backward(projected, slot_weights, gate_saved, up_saved):
     gate_value = gate_saved.astype(jnp.float32)
     up_value = up_saved.astype(jnp.float32)
     sigmoid_gate = jax.nn.sigmoid(gate_value)
@@ -36,20 +33,24 @@
     padded_weights = jnp.concatenate(
         [route_weights.reshape(-1), jnp.zeros((1,), route_weights.dtype)]
     )
-    outgoing = padded_rows[slot_table // slot_count].reshape(experts, capacity, model_width)
+    width = model_width // 128
+    outgoing = padded_rows.reshape(tokens + 1, width, 128)[slot_table // slot_count]
+    outgoing = outgoing.reshape(experts, capacity * width, 128)
     outgoing_weights = padded_weights[slot_table].reshape(experts, capacity)
+    weight_rows = lax.all_gather(down_weight[0], "seq", axis=0, tiled=True)
     arrived, arrived_weights = (
         lax.all_to_all(outgoing, "exp", split_axis=0, concat_axis=0, tiled=True),
         lax.all_to_all(outgoing_weights, "exp", split_axis=0, concat_axis=0, tiled=True),
     )
     local_rows = arrived.reshape(experts * capacity, model_width)
     local_weights = arrived_weights.reshape(-1)
-    all_rows, all_weights = (
-        lax.all_gather(local_rows, "seq", axis=0, tiled=True),
-        lax.all_gather(local_weights, "seq", axis=0, tiled=True),
+    all_weights = lax.all_gather(local_weights, "seq", axis=0, tiled=True)
+    projected = lax.dot_general(
+        weight_rows, local_rows, (((1,), (1,)), ((), ())), preferred_element_type=jnp.float32
     )
+    projected = lax.all_to_all(projected, "seq", split_axis=0, concat_axis=1, tiled=True).T
     grad_gate, grad_up, partial_value = expert_backward(
-        all_rows, all_weights, down_weight[0], gate_pre[0], up_pre[0]
+        projected, all_weights, gate_pre[0], up_pre[0]
     )
     scores = lax.psum_scatter(partial_value, "seq", scatter_dimension=0, tiled=True)
     gate_out = grad_gate.astype(jnp.bfloat16)[None]

time: 424 us -> 280 us (0.66)
  blocking collectives: 221 us -> 23.7 us
  waiting for transfers between devices: 109 us -> 155 us
  starting transfers between devices: 32.1 us -> 53.3 us
  local copies, waits for them, and re-layouts: 33.3 us -> 22.5 us
    all_to_all x1 -> x0, blocking collectives: 204 us -> none  [per_device(): lax.all_to_all(outgoing, 'exp', split_axis=0, concat_axis=0, tiled=True)]
    all_to_all x0 -> x2, waiting for transfers between devices: none -> 136 us  [the longest x1 136 us: per_device(): lax.all_to_all(outgoing, 'exp', split_axis=0, concat_axis=0, tiled=True)]
    all_gather x1, waiting for transfers between devices: 81.6 us -> 0.01 us  [per_device(): weight_rows = lax.all_gather(down_weight[0], 'seq', axis=0, tiled=True)]
    all_to_all x0 -> x2, starting transfers between devices: none -> 24.6 us  [the longest x1 20.4 us: per_device(): lax.all_to_all(outgoing, 'exp', split_axis=0, concat_axis=0, tiled=True)]
    all_to_all x1, waiting for transfers between devices: 12.9 us -> 3.63 us  [per_device(): lax.all_to_all(outgoing_weights, 'exp', split_axis=0, concat_axis=0, tile...]
    reshape x1, local copies, waits for them, and re-layouts: 7.08 us -> 0.18 us  [per_device(): padded_rows.reshape(tokens + 1, width, 128)[slot_table // slot_count]]
    all_gather x1, blocking collectives: 9.82 us -> 16.1 us  [per_device(): all_weights = lax.all_gather(local_weights, 'seq', axis=0, tiled=True)]
  transfers between devices with their start and end apart: 3 -> 5, of which waited for: 3 -> 3; matrix products, arithmetic and copies ran while one was open for 1% -> 6% of each run, Pallas kernels for 0% -> 0%
where the time goes in v1:
time: 280 us
  waiting for transfers between devices  155 us (55%)
  starting transfers between devices  53.3 us (19%)
  blocking collectives  23.7 us (8%)
  local copies, waits for them, and re-layouts  22.5 us (8%)
  between operations  14.9 us (5%)
  matrix products  6.37 us (2%)
  other arithmetic  3.97 us (1%)
    all_to_all x1, waiting for transfers between devices, per_device(): lax.all_to_all(outgoing, 'exp', split_axis=0, concat_axis=0, tiled=True)  136 us
    all_to_all x1, starting transfers between devices, per_device(): lax.all_to_all(outgoing, 'exp', split_axis=0, concat_axis=0, tiled=True)  20.4 us
    all_to_all x1, starting transfers between devices, per_device(): lax.all_to_all(scores.reshape(experts, capacity), 'exp', split_axis=0, co...  17.3 us
    all_gather x1, blocking collectives, per_device(): all_weights = lax.all_gather(local_weights, 'seq', axis=0, tiled=True)  16.1 us
    all_to_all x1, waiting for transfers between devices, per_device(): lax.all_to_all(scores.reshape(experts, capacity), 'exp', split_axis=0, co...  14.8 us
    all_to_all x1, starting transfers between devices, per_device(): lax.all_to_all(outgoing_weights, 'exp', split_axis=0, concat_axis=0, tile...  11.4 us
    unnamed x1, blocking collectives  7.63 us
    dot_general x1, matrix products, per_device(): lax.dot_general(weight_rows, local_rows, (((1,), (1,)), ((), ())), prefer...  6.37 us
  transfers between devices with their start and end apart: 5, of which 3 were waited for; matrix products, arithmetic and copies ran while one was open for 6% of the time, Pallas kernels for 0%

profile of v1, /device:TPU:1, one launch (start us, length us, event | category | flops | bytes accessed | tf_op | source)
XLA Modules:
  0.0 279.9 jit_solution(9235911820327416787)
XLA Ops:
  7.2 0.9 copy.29
  8.3 0.7 broadcast_multiply_fusion
  9.1 0.2 fusion.16
  9.9 1.4 scatter_custom_fusion
  11.4 0.2 copy.39
  11.9 3.2 %gather_fusion.1 = bf16[384,32,128]{2,1,0:T(8,128)(2,1)} fusion(bf16[129,32,128]{2,1,0:T(8,128)(2,1)S(1)} %slice.15, s32[1024]{0:T(1024)S(1)} %get-tuple-element.17), kind=kCustom, calls=%fused_computation.1 | custom fusion | bytes 6292992 | tf_op jit(solution)/shard_map/gather | solution.py:37
  15.1 20.4 %all-to-all-start.1 = ((bf16[128,96,128]{2,1,0:T(8,128)(2,1)}), bf16[128,96,128]{2,1,0:T(8,128)(2,1)S(1)}, u32[]{:S(2)}, u32[]{:S(2)}) async-start(bf16[128,96,128]{2,1,0:T(8,128)(2,1)} %bitcast.64), calls=%async_computation.1 | async-start | bytes 6291456 | tf_op jit(solution)/shard_map/all_to_all | solution.py:42
  35.6 0.7 all-gather.4.cloned.1.call-update
  36.6 2.8 %gather_fusion = bf16[384]{0:T(512)(128)(2,1)S(1)} fusion(bf16[257]{0:T(512)(128)(2,1)S(1)} %pad_maximum_fusion, s32[1024]{0:T(1024)S(1)} %get-tuple-element.18), kind=kCustom, calls=%fused_computation | custom fusion | bytes 3072 | tf_op jit(solution)/shard_map/gather | solution.py:39
  39.4 0.9 all_to_all.38
  40.3 135.9 %all-to-all-done.1 = bf16[128,96,128]{2,1,0:T(8,128)(2,1)S(1)} async-done(((bf16[128,96,128]{2,1,0:T(8,128)(2,1)}), bf16[128,96,128]{2,1,0:T(8,128)(2,1)S(1)}, u32[]{:S(2)}, u32[]{:S(2)}) %all-to-all-start.1) | async-done | bytes 3145760 | tf_op jit(solution)/shard_map/all_to_all | solution.py:42
  176.1 11.4 %all-to-all-start = ((bf16[128,1,3]{2,1,0:T(2,128)(2,1)}), bf16[128,1,3]{2,1,0:T(2,128)(2,1)S(1)}, u32[]{:S(2)}, u32[]{:S(2)}) async-start(bf16[128,1,3]{2,1,0:T(2,128)(2,1)} %all_to_all.38), calls=%async_computation | async-start | bytes 131072 | tf_op jit(solution)/shard_map/all_to_all | solution.py:43
  187.5 3.4 %reshape.96 = bf16[384,4096]{1,0:T(8,128)(2,1)} reshape(bf16[128,96,128]{2,1,0:T(8,128)(2,1)S(1)} %all-to-all-done.1) | data formatting | bytes 6291456 | tf_op jit(solution)/shard_map/reshape | solution.py:45
  191.0 6.4 %fusion.2 = f32[768,384]{0,1:T(8,128)S(1)} fusion(bf16[384,4096]{1,0:T(8,128)(2,1)} %reshape.96, bf16[1,768,4096]{2,1,0:T(8,128)(2,1)} %all-gather.4.cloned.1.call-done), kind=kOutput, calls=%fused_computation.11 | convolution fusion | flops 2415919104 | bytes 10616832 | tf_op jit(solution)/shard_map/dot_general | solution.py:48
  197.4 1.4 copy.34
  198.7 3.6 %all-to-all-done = bf16[128,1,3]{2,1,0:T(2,128)(2,1)S(1)} async-done(((bf16[128,1,3]{2,1,0:T(2,128)(2,1)}), bf16[128,1,3]{2,1,0:T(2,128)(2,1)S(1)}, u32[]{:S(2)}, u32[]{:S(2)}) %all-to-all-start) | async-done | bytes 800 | tf_op jit(solution)/shard_map/all_to_all | solution.py:43
  202.4 4.2 %all-to-all-start.2 = ((f32[4,192,384]{2,1,0:T(8,128)}), f32[4,192,384]{2,1,0:T(8,128)S(1)}, u32[]{:S(2)}, u32[]{:S(2)}) async-start(f32[4,192,384]{2,1,0:T(8,128)} %bitcast.8), calls=%async_computation.2 | async-start | bytes 2359296 | tf_op jit(solution)/shard_map/all_to_all | solution.py:51
  206.5 1.3 dynamic-slice
  208.5 0.2 reduce
  208.7 0.2 reshape.136
  208.9 16.1 %all-gather.1 = bf16[4,1,384]{2,1,0:T(2,128)(2,1)S(1)} all-gather(bf16[1,1,384]{2,1,0:T(2,128)(2,1)S(1)} %reshape.136), channel_id=1, replica_groups=mesh['seq'=4,'exp'=128] {'seq'}, dimensions={0}, use_global_device_ids=true | all-gather | bytes 3840 | tf_op jit(solution)/shard_map/all_gather | solution.py:47
  225.2 0.9 copy-done.1
  226.3 1.8 fusion.9
  228.1 7.6 %all-reduce.1 = f32[1536]{0:T(1024)S(1)} all-reduce(f32[1536]{0:T(1024)S(1)} %get-tuple-element.12), channel_id=3, replica_groups=mesh['seq'=4,'exp'=128] {'seq'}, use_global_device_ids=true, to_apply=%region_5.6.clone | all-reduce | flops 1536 | bytes 12288
  235.8 0.8 all_to_all.36
  236.6 17.3 %all-to-all-start.3 = ((f32[128,1,3]{2,1,0:T(1,128)}), f32[128,1,3]{2,1,0:T(1,128)S(1)}, u32[]{:S(2)}, u32[]{:S(2)}) async-start(f32[128,1,3]{2,1,0:T(1,128)} %bitcast.17), calls=%async_computation.3 | async-start | bytes 131072 | tf_op jit(solution)/shard_map/all_to_all | solution.py:58
  253.9 14.8 %all-to-all-done.3 = f32[128,1,3]{2,1,0:T(1,128)S(1)} async-done(((f32[128,1,3]{2,1,0:T(1,128)}), f32[128,1,3]{2,1,0:T(1,128)S(1)}, u32[]{:S(2)}, u32[]{:S(2)}) %all-to-all-start.3) | async-done | bytes 1568 | tf_op jit(solution)/shard_map/all_to_all | solution.py:58
  268.8 0.5 broadcast.94
  269.3 0.8 reduce.6
  270.1 0.2 reshape.97
  270.3 2.0 gather_fusion.2
  272.4 0.6 copy.37
  (37 shorter events, 2.1 us)
Async XLA Ops:
  7.2 4.2 %copy-start = (bf16[128,4096]{1,0:T(8,128)(2,1)S(1)}, bf16[128,4096]{1,0:T(8,128)(2,1)}, u32[]{:S(2)}) copy-start(bf16[128,4096]{1,0:T(8,128)(2,1)} %param.6) | copy-start | bytes 3145732
  15.1 161.0 %all-to-all-start.1 = ((bf16[128,96,128]{2,1,0:T(8,128)(2,1)}), bf16[128,96,128]{2,1,0:T(8,128)(2,1)S(1)}, u32[]{:S(2)}, u32[]{:S(2)}) async-start(bf16[128,96,128]{2,1,0:T(8,128)(2,1)} %bitcast.64), calls=%async_computation.1 | async-start | bytes 6291456 | tf_op jit(solution)/shard_map/all_to_all | solution.py:42
  35.5 0.8 copy-start.3
  35.5 155.5 %all-gather.4.cloned.1.call-start = ((), (), s32[]{:S(2)}) async-start(), calls=%async_computation.4 | async-start | bytes 7864320 | tf_op jit(solution)/shard_map/all_gather | solution.py:40
  176.1 26.2 %all-to-all-start = ((bf16[128,1,3]{2,1,0:T(2,128)(2,1)}), bf16[128,1,3]{2,1,0:T(2,128)(2,1)S(1)}, u32[]{:S(2)}, u32[]{:S(2)}) async-start(bf16[128,1,3]{2,1,0:T(2,128)(2,1)} %all_to_all.38), calls=%async_computation | async-start | bytes 131072 | tf_op jit(solution)/shard_map/all_to_all | solution.py:43
  202.4 22.7 %all-to-all-start.2 = ((f32[4,192,384]{2,1,0:T(8,128)}), f32[4,192,384]{2,1,0:T(8,128)S(1)}, u32[]{:S(2)}, u32[]{:S(2)}) async-start(f32[4,192,384]{2,1,0:T(8,128)} %bitcast.8), calls=%async_computation.2 | async-start | bytes 2359296 | tf_op jit(solution)/shard_map/all_to_all | solution.py:51
  225.0 1.1 copy-start.1
  225.1 1.2 copy-start.2
  236.6 32.1 %all-to-all-start.3 = ((f32[128,1,3]{2,1,0:T(1,128)}), f32[128,1,3]{2,1,0:T(1,128)S(1)}, u32[]{:S(2)}, u32[]{:S(2)}) async-start(f32[128,1,3]{2,1,0:T(1,128)} %bitcast.17), calls=%async_computation.3 | async-start | bytes 131072 | tf_op jit(solution)/shard_map/all_to_all | solution.py:58
Sparse Core Ops, SparseCore 0:
  38.5 74.3 all-gather.3

commit v2 on v0

v2 whole, which is shorter than its diff:
```python
import functools

import jax
import jax.numpy as jnp
from jax import lax
from jax.experimental import pallas as pl
from jax.experimental.pallas import tpu as pltpu
from jax.sharding import PartitionSpec as P

MESH = pl.DeviceIdType.MESH
WINDOW = 4
SEQ, ZN, PLANE = 4, 16, 8
SELF = 12
EXT = 128
F32, BF16 = jnp.float32, jnp.bfloat16
FAR = (4, 3, 5, 2, 6, 1, 7)
ALL_THIRD = (4, 3, 5, 2, 6, 1, 7, 0, 8, 9, 15, 10, 14, 11, 13)


def iota(shape, dim):
    return lax.broadcasted_iota(jnp.int32, shape, dim)


def hot(cond):
    return jnp.where(cond, 1.0, 0.0).astype(BF16)


def mm(a, b):
    return jnp.dot(a, b, preferred_element_type=F32)


def mm_t(a, b):
    return lax.dot_general(a, b, (((1,), (1,)), ((), ())), preferred_element_type=F32)


def kernel(
    x_ref, ids_ref, rw_ref, w_ref, g_ref, u_ref,
    gg_ref, gu_ref, rg_ref,
    s_main, r_main, s_third, r_third, t_main, x_main, t_third, x_third,
    w_all, g_all, u_all, g_perm, u_perm, acc, grads, back,
    score, score_in, total, total_in,
    z_s, z_r, zt_s, zt_r, p_s, p_r, y_s, y_r, b_s, b_r, ps_s, ps_r, zs_s, zs_r, local_sem,
):
    width = x_ref.shape[1]
    ff = w_ref.shape[0]
    block = g_ref.shape[1] // SEQ
    wide = width + EXT
    half = width // 2
    step = width // 4
    pieces = [(0, EXT + step)] + [(EXT + step * n, step) for n in range(1, 4)]

    s = lax.axis_index("seq")
    e = lax.axis_index("exp")
    z, x, c = e >> 3, (e >> 1) & 3, e & 1

    def z_to(k):
        return (s, (((z - 4 - k) & 15) << 3) | (e & 7))

    def z_from(k):
        return (s, (((z + 4 + k) & 15) << 3) | (e & 7))

    def p_to(j):
        return (s, (z << 3) | (((x + (j >> 1)) & 3) << 1) | ((c + (j & 1)) & 1))

    def p_from(j):
        return (s, (z << 3) | (((x - (j >> 1)) & 3) << 1) | ((c + (j & 1)) & 1))

    def y_to(q):
        return ((s + q) & 3, e)

    def y_from(q):
        return ((s - q) & 3, e)

    def remote(src, dst, send, recv, device):
        return pltpu.make_async_remote_copy(
            src_ref=src, dst_ref=dst, send_sem=send, recv_sem=recv,
            device_id=device, device_id_type=MESH,
        )

    barrier = pltpu.get_barrier_semaphore()
    for k in range(ZN):
        if k != SELF:
            pl.semaphore_signal(barrier, inc=1, device_id=z_from(k), device_id_type=MESH)
    for j in range(1, PLANE):
        pl.semaphore_signal(barrier, inc=1, device_id=p_from(j), device_id_type=MESH)
    for q in range(1, SEQ):
        pl.semaphore_signal(barrier, inc=1, device_id=y_from(q), device_id_type=MESH)

    own_w = pltpu.make_async_copy(w_ref, w_all.at[pl.ds(0, ff)], local_sem)
    own_w.start()

    ids0, ids1 = ids_ref[0:1, :], ids_ref[1:2, :]
    w0, w1 = rw_ref[0:1, :], rw_ref[1:2, :]
    tokens = ids_ref.shape[1]
    earlier = hot(iota((tokens, tokens), 0) < iota((tokens, tokens), 1))
    row = iota((256, tokens), 0)
    lane = iota((256, tokens), 1)
    expert = (((z - 4 - (row >> 4)) & 15) << 3) | (row & 7)
    upper = (row >> 3) & 1
    named0 = ids0 == expert
    named = named0 | (ids1 == expert)
    rank = mm(hot(named), earlier)
    is_main = named & (rank == upper.astype(F32))
    is_third = named & (rank == 2.0)
    m_main = hot(is_main)
    m_low, m_high = hot(is_third & (upper == 0)), hot(is_third & (upper == 1))
    value = jnp.where(named0, w0, w1)
    v_main = jnp.sum(jnp.where(is_main, value, 0.0), axis=1, keepdims=True)
    v_third = jnp.sum(jnp.where(is_third, value, 0.0), axis=1, keepdims=True)
    s_main[:, 0:EXT] = jnp.where(
        lane == 0, v_main, jnp.where(lane == 1, v_third, 0.0)
    ).astype(BF16)

    score[...] = jnp.zeros((8, 128), F32)
    own_w.wait()
    pl.semaphore_wait(barrier, ZN - 1 + PLANE - 1 + SEQ - 1)

    y_copies = []
    for q in range(1, SEQ):
        rows = pl.ds(ff * q, ff)
        lanes = pl.ds(pl.multiple_of(((s + q) & 3) * block, 128), block)
        y_copies.append([
            remote(g_ref.at[:, lanes], g_all.at[rows], y_s.at[0, q], y_r.at[0, q], y_to(q)),
            remote(u_ref.at[:, lanes], u_all.at[rows], y_s.at[1, q], y_r.at[1, q], y_to(q)),
            remote(w_all.at[pl.ds(0, ff)], w_all.at[rows], y_s.at[2, q], y_r.at[2, q], y_to(q)),
        ])

    pending = []

    def issue(copy):
        if len(pending) >= WINDOW:
            pending.pop(0).wait_send()
        copy.start()
        pending.append(copy)

    def main_copy(k, start, size, n):
        part = (pl.ds(16 * k, 16), pl.ds(start, size))
        return remote(s_main.at[part], r_main.at[part], z_s.at[k, n], z_r.at[k, n], z_to(k))

    whole = {k: main_copy(k, 0, wide, 0) for k in (8, 9, 15, 10, 14, 11, 13, 0)}
    part = {
        (k, n): main_copy(k, start, size, n) for n, (start, size) in enumerate(pieces) for k in FAR
    }
    third = {
        k: remote(
            s_third.at[pl.ds(16 * k, 16)], r_third.at[pl.ds(16 * k, 16)],
            zt_s.at[k], zt_r.at[k], z_to(k),
        )
        for k in ALL_THIRD
    }

    for start in range(0, width, 1024):
        s_main[128:256, EXT + start : EXT + start + 1024] = mm(
            m_main[128:256], x_ref[:, start : start + 1024]
        ).astype(BF16)
    for k in (8, 9, 15, 10):
        issue(whole[k])
    for n in (0, 1, 2):
        for q in range(1, SEQ):
            y_copies[q - 1][n].start()
    for start in range(0, width, 1024):
        s_main[0:128, EXT + start : EXT + start + 1024] = mm(
            m_main[0:128], x_ref[:, start : start + 1024]
        ).astype(BF16)
    for start in range(0, half, 1024):
        s_third[:, start : start + 1024] = (
            mm(m_low, x_ref[:, start : start + 1024])
            + mm(m_high, x_ref[:, half + start : half + start + 1024])
        ).astype(BF16)
    for k in (14, 0, 11, 13):
        issue(whole[k])
    r_main[16 * SELF : 16 * SELF + 16, :] = s_main[16 * SELF : 16 * SELF + 16, :]
    r_third[16 * SELF : 16 * SELF + 16, :] = s_third[16 * SELF : 16 * SELF + 16, :]

    out_row = iota((128, 128), 0)
    j_of = out_row >> 4
    p_of = (((x + (j_of >> 1)) & 3) << 1) | ((c + (j_of & 1)) & 1)
    regroup = hot(
        iota((128, 128), 1) == ((out_row >> 1) & 7) * 16 + (out_row & 1) * 8 + p_of
    )
    out_row = iota((128, 256), 0)
    j_of = out_row >> 4
    p_of = (((x + (j_of >> 1)) & 3) << 1) | ((c + (j_of & 1)) & 1)
    low_row = (out_row & 15) * 16 + p_of
    regroup_low = hot(iota((128, 256), 1) == low_row)
    regroup_high = hot(iota((128, 256), 1) == low_row + 8)

    plane_copies = []

    def plane_send(src, dst, start, size, n):
        group = []
        for j in range(1, PLANE):
            area = (pl.ds(16 * j, 16), pl.ds(start, size))
            copy = remote(src.at[area], dst.at[area], p_s.at[n, j], p_r.at[n, j], p_to(j))
            copy.start()
            group.append(copy)
        plane_copies.extend(group)
        dst[0:16, start : start + size] = src[0:16, start : start + size]
        return group

    def split(start, size):
        at = start
        while at < start + size:
            span = min(1152, start + size - at)
            yield at, span
            at += span

    def main_forward(h, start, size, n):
        base = 128 if h == 0 else 0
        for at, span in split(start, size):
            t_main[h, :, at : at + span] = mm(
                regroup, r_main[base : base + 128, at : at + span]
            ).astype(BF16)
        return plane_send(t_main.at[h], x_main.at[h], start, size, n)

    def third_forward(n):
        for at, span in split(0, half):
            rows = r_third[:, at : at + span]
            t_third[:, at : at + span] = mm(regroup_low, rows).astype(BF16)
            t_third[:, half + at : half + at + span] = mm(regroup_high, rows).astype(BF16)
        return plane_send(t_third, x_third, 0, width, n)

    def natural(index):
        chunk, low = index >> 7, index & 127
        j = low >> 4
        is3 = chunk == 1
        k = jnp.where(is3, low & 15, ((low >> 1) & 7) + jnp.where(chunk == 0, 8, 0))
        r = jnp.where(is3, 2, low & 1)
        source = (((x - (j >> 1)) & 3) << 1) | ((c + (j & 1)) & 1)
        return ((z + 4 + k) & 15) * 24 + source * 3 + r

    def gates_ready():
        own = pl.ds(pl.multiple_of(s * block, 128), block)
        g_all[0:ff, :] = g_ref[:, own]
        u_all[0:ff, :] = u_ref[:, own]
        order = hot(iota((block, block), 0) == natural(iota((block, block), 1)))
        for q in range(SEQ):
            if q:
                y_copies[q - 1][0].wait_recv()
                y_copies[q - 1][1].wait_recv()
            rows = slice(ff * q, ff * q + ff)
            g_perm[rows, :] = mm(g_all[rows, :], order).astype(BF16)
            u_perm[rows, :] = mm(u_all[rows, :], order).astype(BF16)

    back_copies = []

    def finish(chunk, weights):
        lanes = slice(128 * chunk, 128 * chunk + 128)
        summed = jnp.zeros((1, 128), F32)
        for q in (2, 1, 3, 0):
            rows = slice(ff * q, ff * q + ff)
            projected = acc[rows, :]
            gate = g_perm[rows, lanes].astype(F32)
            up = u_perm[rows, lanes].astype(F32)
            sig = jax.nn.sigmoid(gate)
            activated = gate * sig
            summed = summed + jnp.sum(activated * up * projected, axis=0, keepdims=True)
            scaled = weights * projected
            grad_up = (scaled * activated).astype(BF16)
            grad_gate = (scaled * up * sig * (1.0 + gate * (1.0 - sig))).astype(BF16)
            if q:
                grads[chunk, rows, 0:128] = grad_gate
                grads[chunk, rows, 128:256] = grad_up
                copy = remote(
                    grads.at[chunk, pl.ds(ff * q, ff)], back.at[chunk, q],
                    b_s.at[chunk, q], b_r.at[chunk, q], y_from(q),
                )
                copy.start()
                back_copies.append(copy)
            else:
                back[chunk, 0, :, 0:128] = grad_gate
                back[chunk, 0, :, 128:256] = grad_up
        score[chunk : chunk + 1, :] = summed

    def slot_weights(h):
        pick = hot(iota((16, 128), 0) == iota((16, 128), 1))
        return mm_t(pick, x_main[h, :, 0:EXT])

    def spread(weights, h):
        src, dst = iota((128, 128), 0), iota((128, 128), 1)
        match = (src & 1 == 0) & (src >> 4 == dst >> 4)
        match = match & (dst & 15 == ((src >> 1) & 7) + (8 if h == 0 else 0))
        return mm(weights.astype(BF16), hot(match))

    for k in ALL_THIRD[:5]:
        issue(third[k])
    for k in (8, 9, 15, 10, 14, 11, 13):
        whole[k].wait_recv()
    near_group = main_forward(0, 0, wide, 0)
    for k in ALL_THIRD[5:9]:
        issue(third[k])
    gates_ready()
    for k in ALL_THIRD[9:]:
        issue(third[k])
    for k in FAR[:4]:
        issue(part[k, 0])
    for k in ALL_THIRD:
        third[k].wait_recv()
    third_group = third_forward(1)
    for k in FAR[4:]:
        issue(part[k, 0])
    for group in y_copies:
        group[2].wait_recv()
    for copy in near_group:
        copy.wait_recv()
    acc[...] = mm_t(w_all[...], x_main[0, :, EXT:])
    near_weights = slot_weights(0)
    finish(0, near_weights[0:1, :])
    far_groups = []

    def far_forward(n):
        if n == 0:
            whole[0].wait_recv()
        for k in FAR:
            part[k, n].wait_recv()
        far_groups.append(main_forward(1, pieces[n][0], pieces[n][1], 2 + n))

    def far_product(n):
        for copy in far_groups[n]:
            copy.wait_recv()
        product = mm_t(
            w_all[:, step * n : step * n + step],
            x_main[1, :, EXT + step * n : EXT + step * n + step],
        )
        if n == 0:
            acc[...] = product
        else:
            acc[...] += product

    for k in FAR[:4]:
        issue(part[k, 1])
    far_forward(0)
    for k in FAR[4:]:
        issue(part[k, 1])
    for copy in third_group:
        copy.wait_recv()
    acc[...] = mm_t(w_all[...], x_third[...])
    for copy in far_groups[0]:
        copy.wait_recv()
    far_weights = slot_weights(1)
    third_weights = spread(near_weights, 0) + spread(far_weights, 1)
    finish(1, third_weights[1:2, :])
    for k in FAR[:4]:
        issue(part[k, 2])
    far_forward(1)
    acc[...] = mm_t(w_all[:, 0:step], x_main[1, :, EXT : EXT + step])
    for k in FAR[4:]:
        issue(part[k, 2])
    for k in FAR[:4]:
        issue(part[k, 3])
    far_forward(2)
    far_product(1)
    for k in FAR[4:]:
        issue(part[k, 3])
    far_product(2)
    far_forward(3)
    far_product(3)
    finish(2, far_weights[0:1, :])

    score_copies = []
    for j in range(1, PLANE):
        copy = remote(score, score_in.at[j], ps_s.at[j], ps_r.at[j], p_from(j))
        copy.start()
        score_copies.append(copy)
    place = iota((8, 128), 1)
    gathered = jnp.where(place >> 4 == 0, score[...], 0.0)
    for j in range(1, PLANE):
        score_copies[j - 1].wait_recv()
        gathered = jnp.where(place >> 4 == j, score_in[j], gathered)
    total[...] = gathered
    total_copies = {}
    for k in FAR + (0, 8, 9, 15, 10, 14, 11, 13):
        copy = remote(total, total_in.at[k], zs_s.at[k], zs_r.at[k], z_from(k))
        copy.start()
        total_copies[k] = copy

    restore = hot(natural(iota((block, block), 0)) == iota((block, block), 1))
    for copy in back_copies:
        copy.wait_recv()
    for q in range(SEQ):
        lanes = pl.ds(pl.multiple_of(((s + q) & 3) * block, 128), block)
        for ref, first in ((gg_ref, 0), (gu_ref, 128)):
            value = jnp.concatenate([back[n, q, :, first : first + 128] for n in range(3)], axis=1)
            ref[:, lanes] = mm(value, restore).astype(BF16)

    is3 = iota((8, 128), 0) == 1
    low = (place >> 1) & 7
    is_near = iota((8, 128), 0) == 0
    slot = jnp.where(is3, place & 15, jnp.where(is_near, low + 8, low))
    found = jnp.where(slot == SELF, total[...], 0.0)
    for k in FAR + (0, 8, 9, 15, 10, 14, 11, 13):
        total_copies[k].wait_recv()
        found = jnp.where(slot == k, total_in[k], found)
    columns = jnp.transpose(jnp.concatenate([found, jnp.zeros((120, 128), F32)], axis=0))
    row = iota((128, 128), 0)
    j = row >> 4
    target = (((x + (j >> 1)) & 3) << 1) | ((c + (j & 1)) & 1)
    result0 = jnp.zeros((1, 128), F32)
    result1 = jnp.zeros((1, 128), F32)
    for chunk in range(3):
        if chunk == 1:
            k, r = row & 15, jnp.full((128, 128), 2, jnp.int32)
        else:
            k, r = ((row >> 1) & 7) + (8 if chunk == 0 else 0), row & 1
        expert = (((z - 4 - k) & 15) << 3) | target
        first, second = ids0 == expert, ids1 == expert
        match = mm(hot(first | second), earlier) == r.astype(F32)
        column = columns[:, chunk : chunk + 1]
        result0 += jnp.sum(jnp.where(first & match, column, 0.0), axis=0, keepdims=True)
        result1 += jnp.sum(jnp.where(second & match, column, 0.0), axis=0, keepdims=True)
    rg_ref[0:1, :] = result0
    rg_ref[1:2, :] = result1

    for copy in pending + plane_copies + back_copies + score_copies + list(total_copies.values()):
        copy.wait_send()
    for group in y_copies:
        for copy in group:
            copy.wait_send()


def per_device(out_grad, expert_ids, route_weights, down_weight, gate_pre, up_pre):
    tokens, width = out_grad.shape
    ff = down_weight.shape[1]
    rows = gate_pre.shape[1]
    block = rows // SEQ
    wide = width + EXT
    vmem = pl.BlockSpec(memory_space=pltpu.VMEM)
    dma = pltpu.SemaphoreType.DMA
    gate_out, up_out, route = pl.pallas_call(
        kernel,
        out_shape=(
            jax.ShapeDtypeStruct((ff, rows), BF16),
            jax.ShapeDtypeStruct((ff, rows), BF16),
            jax.ShapeDtypeStruct((2, tokens), F32),
        ),
        in_specs=[vmem, vmem, vmem, pl.BlockSpec(memory_space=pl.ANY), vmem, vmem],
        out_specs=(vmem, vmem, vmem),
        scratch_shapes=[
            pltpu.VMEM((256, wide), BF16),
            pltpu.VMEM((256, wide), BF16),
            pltpu.VMEM((256, width // 2), BF16),
            pltpu.VMEM((256, width // 2), BF16),
            pltpu.VMEM((2, 128, wide), BF16),
            pltpu.VMEM((2, 128, wide), BF16),
            pltpu.VMEM((128, width), BF16),
            pltpu.VMEM((128, width), BF16),
            pltpu.VMEM((SEQ * ff, width), BF16),
            pltpu.VMEM((SEQ * ff, block), BF16),
            pltpu.VMEM((SEQ * ff, block), BF16),
            pltpu.VMEM((SEQ * ff, block), BF16),
            pltpu.VMEM((SEQ * ff, block), BF16),
            pltpu.VMEM((SEQ * ff, 128), F32),
            pltpu.VMEM((3, SEQ * ff, 256), BF16),
            pltpu.VMEM((3, SEQ, ff, 256), BF16),
            pltpu.VMEM((8, 128), F32),
            pltpu.VMEM((PLANE, 8, 128), F32),
            pltpu.VMEM((8, 128), F32),
            pltpu.VMEM((ZN, 8, 128), F32),
            dma((ZN, 4)), dma((ZN, 4)), dma((ZN,)), dma((ZN,)),
            dma((6, PLANE)), dma((6, PLANE)), dma((3, SEQ)), dma((3, SEQ)),
            dma((3, SEQ)), dma((3, SEQ)), dma((PLANE,)), dma((PLANE,)),
            dma((ZN,)), dma((ZN,)), dma,
        ],
        compiler_params=pltpu.CompilerParams(
            collective_id=0, has_side_effects=True, vmem_limit_bytes=56 * 2**20
        ),
        cost_estimate=pl.CostEstimate(
            flops=2 * SEQ * ff * width * block, bytes_accessed=8 * 2**20, transcendentals=0
        ),
        name="expert_backward",
    )(
        out_grad,
        expert_ids.T,
        route_weights.T.astype(F32),
        down_weight[0],
        gate_pre[0].T,
        up_pre[0].T,
    )
    return gate_out.T[None], up_out.T[None], route.T


def solution(mesh):
    placed = (
        P(("seq", "exp"), None),
        P(("seq", "exp"), None),
        P(("seq", "exp"), None),
        P("exp", "seq", None),
        P("exp", None, "seq"),
        P("exp", None, "seq"),
    )
    return jax.shard_map(
        per_device,
        mesh=mesh,
        in_specs=placed,
        out_specs=(P("exp", None, "seq"), P("exp", None, "seq"), P(("seq", "exp"), None)),
        check_vma=False,
    )
```

time: 424 us -> 197 us (0.46)
  blocking collectives: 221 us -> 0 us
  Pallas kernels: 0 us -> 192 us
  waiting for transfers between devices: 109 us -> 0 us
  starting transfers between devices: 32.1 us -> 0 us
  local copies, waits for them, and re-layouts: 33.3 us -> 3.36 us
  between operations: 14.9 us -> 0.66 us
  matrix products: 10.4 us -> 0 us
    all_to_all x1 -> x0, blocking collectives: 204 us -> none  [per_device(): lax.all_to_all(outgoing, 'exp', split_axis=0, concat_axis=0, tiled=True)]
    pallas_call x0 -> x1, Pallas kernels: none -> 192 us  [per_device(): pl.pallas_call(kernel, out_shape=(jax.ShapeDtypeStruct((ff, rows), BF16),...]
    all_gather x1 -> x0, waiting for transfers between devices: 81.6 us -> none  [per_device(): lax.all_gather(local_rows, 'seq', axis=0, tiled=True)]
    all_to_all x2 -> x0, starting transfers between devices: 32 us -> none  [the longest x1 18.9 us: per_device(): lax.all_to_all(scores.reshape(experts, capacity), 'exp', split_axis=0, co...]
    all_to_all x2 -> x0, waiting for transfers between devices: 27.7 us -> none  [the longest x1 14.8 us: per_device(): lax.all_to_all(scores.reshape(experts, capacity), 'exp', split_axis=0, co...]
    reshape x5 -> x0, local copies, waits for them, and re-layouts: 15 us -> none  [the longest x1 7.44 us: per_device(): local_rows = arrived.reshape(experts * capacity, model_width)]
    dot_general x1 -> x0, matrix products: 10.4 us -> none  [expert_backward(): lax.dot_general(slot_rows, down_rows, (((1,), (1,)), ((), ())), preferred...]
    all_gather x1 -> x0, blocking collectives: 9.82 us -> none  [per_device(): lax.all_gather(local_weights, 'seq', axis=0, tiled=True)]
  transfers between devices with their start and end apart: 3 -> 0, of which waited for: 3 -> 0; matrix products, arithmetic and copies ran while one was open for 1% -> 0% of each run, Pallas kernels for 0% -> 0%
where the time goes in v2:
time: 197 us
  Pallas kernels  192 us (97%)
  local copies, waits for them, and re-layouts  3.36 us (2%)
    pallas_call x1, Pallas kernels, per_device(): pl.pallas_call(kernel, out_shape=(jax.ShapeDtypeStruct((ff, rows), BF16),...  192 us

profile of v2, /device:TPU:1, one launch (start us, length us, event | category | flops | bytes accessed | tf_op | source)
XLA Modules:
  0.0 197.2 jit_solution(2199023483451536272)
XLA Ops:
  0.6 1.2 convert_bitcast_fusion.rw_ref
  1.8 192.0 %expert_backward.1 = (bf16[192,1536]{1,0:T(8,128)(2,1)}, bf16[192,1536]{1,0:T(8,128)(2,1)}, f32[2,128]{1,0:T(2,128)}) custom-call(bf16[128,4096]{1,0:T(8,128)(2,1)} %x_ref.1, s32[2,128]{1,0:T(2,128)} %bitcast.23, f32[2,128]{1,0:T(2,128)} %convert_bitcast_fusion.rw_ref, bf16[192,4096]{1,0:T(8,128)(2,1)} %bitcast.20, bf16[192,1536]{1,0:T(8,128)(2,1)} %bitcast.21, ...), custom_call_target="tpu_custom_call" | custom-call | flops 2415919104 | bytes 8388608 | tf_op jit(solution)/shard_map/expert_backward/pallas_call | solution.py:429
  193.8 0.0 copy-start
  193.8 0.0 copy-start.1
  193.8 2.0 %copy.12 = bf16[1,1536,192]{1,2,0:T(8,128)(2,1)} copy(bf16[1,1536,192]{1,2,0:T(8,128)(2,1)} %bitcast.18) | data formatting | bytes 1179648
  195.8 0.0 copy-done
  195.8 0.8 copy.13
  196.6 0.0 copy-done.1
  196.6 0.6 copy.14
Async XLA Ops:
  193.8 2.0 %copy-start = (bf16[192,1536]{1,0:T(8,128)(2,1)S(1)}, bf16[192,1536]{1,0:T(8,128)(2,1)}, u32[]{:S(2)}) copy-start(bf16[192,1536]{1,0:T(8,128)(2,1)} %get-tuple-element.7) | copy-start | bytes 1769476
  193.8 2.8 %copy-start.1 = (f32[2,128]{1,0:T(2,128)S(1)}, f32[2,128]{1,0:T(2,128)}, u32[]{:S(2)}) copy-start(f32[2,128]{1,0:T(2,128)} %get-tuple-element.8) | copy-start | bytes 3076

commit v3 on v2

--- a/solution.py
+++ b/solution.py
@@ -8,7 +8,8 @@
 from jax.sharding import PartitionSpec as P
 
 MESH = pl.DeviceIdType.MESH
-WINDOW = 4
+WINDOW = 8
+PIECES = 4
 SEQ, ZN, PLANE = 4, 16, 8
 SELF = 12
 EXT = 128
@@ -34,20 +35,21 @@
 
 
 def kernel(
-    x_ref, ids_ref, rw_ref, w_ref, g_ref, u_ref,
-    gg_ref, gu_ref, rg_ref,
+    spare, x_ref, ids_ref, rw_ref, w_ref, g_ref, u_ref,
+    gg_ref, gu_ref, rg_ref, over_ref,
     s_main, r_main, s_third, r_third, t_main, x_main, t_third, x_third,
     w_all, g_all, u_all, g_perm, u_perm, acc, grads, back,
-    score, score_in, total, total_in,
-    z_s, z_r, zt_s, zt_r, p_s, p_r, y_s, y_r, b_s, b_r, ps_s, ps_r, zs_s, zs_r, local_sem,
+    score, score_in, total, total_in, over, over_in,
+    z_s, z_r, zt_s, zt_r, p_s, p_r, y_s, y_r, b_s, b_r, ps_s, ps_r, zs_s, zs_r, o_s, o_r, local_sem,
 ):
     width = x_ref.shape[1]
     ff = w_ref.shape[0]
     block = g_ref.shape[1] // SEQ
     wide = width + EXT
-    half = width // 2
-    step = width // 4
-    pieces = [(0, EXT + step)] + [(EXT + step * n, step) for n in range(1, 4)]
+    parts = 16 // spare
+    span3 = width // parts
+    step = width // PIECES
+    pieces = [(EXT + step * n, step) for n in range(PIECES)]
 
     s = lax.axis_index("seq")
     e = lax.axis_index("exp")
@@ -90,7 +92,7 @@
     own_w.start()
 
     ids0, ids1 = ids_ref[0:1, :], ids_ref[1:2, :]
-    w0, w1 = rw_ref[0:1, :], rw_ref[1:2, :]
+    w0, w1 = rw_ref[0:1, :].astype(F32), rw_ref[1:2, :].astype(F32)
     tokens = ids_ref.shape[1]
     earlier = hot(iota((tokens, tokens), 0) < iota((tokens, tokens), 1))
     row = iota((256, tokens), 0)
@@ -103,12 +105,29 @@
     is_main = named & (rank == upper.astype(F32))
     is_third = named & (rank == 2.0)
     m_main = hot(is_main)
-    m_low, m_high = hot(is_third & (upper == 0)), hot(is_third & (upper == 1))
+    m_third = hot(is_third)
+    have = mm_t(jnp.ones((16, tokens), BF16), m_third)
+    src, dst = iota((256, 256), 0), iota((256, 256), 1)
+    before = (src >> 4 == dst >> 4) & (src & 8 == 0)
+    ahead = mm(have.astype(BF16), hot(before & (src & 7 < dst & 7)))
+    held = mm(have.astype(BF16), hot(before))
+    excess = jnp.max(jnp.where(held > spare, 1.0, 0.0))
+    packed = (src >> 4 == dst >> 4) & (dst & 8 == 0)
+    packed = packed & (ahead[0:1, :] == (src & (spare - 1)).astype(F32))
+    m_packed = mm(hot(packed), m_third)
+    part_of = (row & 15) >> (spare.bit_length() - 1)
+    m_part = [hot((m_packed > 0.5) & (part_of == n)) for n in range(parts)]
+    rank_in = mm(hot((src >> 4 == dst >> 4) & (dst & 8 == 0) & (dst & 7 < src & 7)), m_third)
+    v_spot = jnp.sum(rank_in, axis=1, keepdims=True)
+    v_have = jnp.sum(m_third.astype(F32), axis=1, keepdims=True)
+    v_spot = jnp.where((v_have > 0.5) & (v_spot < spare - 0.5), v_spot + 1.0, 0.0)
     value = jnp.where(named0, w0, w1)
     v_main = jnp.sum(jnp.where(is_main, value, 0.0), axis=1, keepdims=True)
     v_third = jnp.sum(jnp.where(is_third, value, 0.0), axis=1, keepdims=True)
     s_main[:, 0:EXT] = jnp.where(
-        lane == 0, v_main, jnp.where(lane == 1, v_third, 0.0)
+        lane == 0,
+        v_main,
+        jnp.where(lane == 1, v_third, jnp.where(lane == 2, v_spot, jnp.where(lane == 3, excess, 0.0))),
     ).astype(BF16)
 
     score[...] = jnp.zeros((8, 128), F32)
@@ -141,6 +160,7 @@
     part = {
         (k, n): main_copy(k, start, size, n) for n, (start, size) in enumerate(pieces) for k in FAR
     }
+    extra = {k: main_copy(k, 0, EXT, PIECES) for k in FAR}
     third = {
         k: remote(
             s_third.at[pl.ds(16 * k, 16)], r_third.at[pl.ds(16 * k, 16)],
@@ -162,11 +182,10 @@
         s_main[0:128, EXT + start : EXT + start + 1024] = mm(
             m_main[0:128], x_ref[:, start : start + 1024]
         ).astype(BF16)
-    for start in range(0, half, 1024):
-        s_third[:, start : start + 1024] = (
-            mm(m_low, x_ref[:, start : start + 1024])
-            + mm(m_high, x_ref[:, half + start : half + start + 1024])
-        ).astype(BF16)
+    packed_rows = mm(m_part[0], x_ref[:, 0:span3])
+    for n in range(1, parts):
+        packed_rows += mm(m_part[n], x_ref[:, span3 * n : span3 * n + span3])
+    s_third[...] = packed_rows.astype(BF16)
     for k in (14, 0, 11, 13):
         issue(whole[k])
     r_main[16 * SELF : 16 * SELF + 16, :] = s_main[16 * SELF : 16 * SELF + 16, :]
@@ -178,13 +197,6 @@
     regroup = hot(
         iota((128, 128), 1) == ((out_row >> 1) & 7) * 16 + (out_row & 1) * 8 + p_of
     )
-    out_row = iota((128, 256), 0)
-    j_of = out_row >> 4
-    p_of = (((x + (j_of >> 1)) & 3) << 1) | ((c + (j_of & 1)) & 1)
-    low_row = (out_row & 15) * 16 + p_of
-    regroup_low = hot(iota((128, 256), 1) == low_row)
-    regroup_high = hot(iota((128, 256), 1) == low_row + 8)
-
     plane_copies = []
 
     def plane_send(src, dst, start, size, n):
@@ -214,10 +226,17 @@
         return plane_send(t_main.at[h], x_main.at[h], start, size, n)
 
     def third_forward(n):
-        for at, span in split(0, half):
-            rows = r_third[:, at : at + span]
-            t_third[:, at : at + span] = mm(regroup_low, rows).astype(BF16)
-            t_third[:, half + at : half + at + span] = mm(regroup_high, rows).astype(BF16)
+        out_row = iota((128, 256), 0)
+        column = iota((128, 256), 1)
+        j = out_row >> 4
+        p = (((x + (j >> 1)) & 3) << 1) | ((c + (j & 1)) & 1)
+        chosen = mm(hot(column == (out_row & 15) * 16 + p), r_main[:, 0:EXT])
+        spot = chosen[:, 2:3] - 1.0
+        spot = (out_row & 15 == column >> 4) & (spot == (column & (spare - 1)).astype(F32))
+        part_of = (column & 15) >> (spare.bit_length() - 1)
+        for m in range(parts):
+            match = hot(spot & (part_of == m))
+            t_third[:, span3 * m : span3 * m + span3] = mm(match, r_third[...]).astype(BF16)
         return plane_send(t_third, x_third, 0, width, n)
 
     def natural(index):
@@ -282,23 +301,25 @@
         match = match & (dst & 15 == ((src >> 1) & 7) + (8 if h == 0 else 0))
         return mm(weights.astype(BF16), hot(match))
 
-    for k in ALL_THIRD[:5]:
+    for k in ALL_THIRD[:7]:
+        issue(extra[k])
         issue(third[k])
     for k in (8, 9, 15, 10, 14, 11, 13):
         whole[k].wait_recv()
     near_group = main_forward(0, 0, wide, 0)
-    for k in ALL_THIRD[5:9]:
+    for k in ALL_THIRD[7:]:
         issue(third[k])
     gates_ready()
-    for k in ALL_THIRD[9:]:
-        issue(third[k])
-    for k in FAR[:4]:
+    for k in FAR:
         issue(part[k, 0])
+    for k in FAR:
+        extra[k].wait_recv()
     for k in ALL_THIRD:
         third[k].wait_recv()
+    whole[0].wait_recv()
     third_group = third_forward(1)
-    for k in FAR[4:]:
-        issue(part[k, 0])
+    for k in FAR[:4]:
+        issue(part[k, 1])
     for group in y_copies:
         group[2].wait_recv()
     for copy in near_group:
@@ -309,11 +330,12 @@
     far_groups = []
 
     def far_forward(n):
-        if n == 0:
-            whole[0].wait_recv()
         for k in FAR:
             part[k, n].wait_recv()
-        far_groups.append(main_forward(1, pieces[n][0], pieces[n][1], 2 + n))
+        start, size = pieces[n]
+        if n == 0:
+            start, size = 0, EXT + size
+        far_groups.append(main_forward(1, start, size, 2 + n))
 
     def far_product(n):
         for copy in far_groups[n]:
@@ -327,8 +349,6 @@
         else:
             acc[...] += product
 
-    for k in FAR[:4]:
-        issue(part[k, 1])
     far_forward(0)
     for k in FAR[4:]:
         issue(part[k, 1])
@@ -338,6 +358,15 @@
     for copy in far_groups[0]:
         copy.wait_recv()
     far_weights = slot_weights(1)
+    seen = jnp.maximum(x_main[0, :, 0:EXT].astype(F32), x_main[1, :, 0:EXT].astype(F32))
+    seen = jnp.max(seen, axis=0, keepdims=True)
+    seen = jnp.max(jnp.where(iota((1, 128), 1) == 3, seen, 0.0), axis=1, keepdims=True)
+    over[...] = jnp.broadcast_to(seen, (8, 128))
+    over_copies = []
+    for q in range(1, SEQ):
+        copy = remote(over, over_in.at[q], o_s.at[q], o_r.at[q], y_to(q))
+        copy.start()
+        over_copies.append(copy)
     third_weights = spread(near_weights, 0) + spread(far_weights, 1)
     finish(1, third_weights[1:2, :])
     for k in FAR[:4]:
@@ -382,6 +411,12 @@
         for ref, first in ((gg_ref, 0), (gu_ref, 128)):
             value = jnp.concatenate([back[n, q, :, first : first + 128] for n in range(3)], axis=1)
             ref[:, lanes] = mm(value, restore).astype(BF16)
+
+    worst = over[...]
+    for q in range(1, SEQ):
+        over_copies[q - 1].wait_recv()
+        worst = jnp.maximum(worst, over_in[q])
+    over_ref[0, 0] = jnp.max(worst).astype(jnp.int32)
 
     is3 = iota((8, 128), 0) == 1
     low = (place >> 1) & 7
@@ -411,14 +446,16 @@
     rg_ref[0:1, :] = result0
     rg_ref[1:2, :] = result1
 
-    for copy in pending + plane_copies + back_copies + score_copies + list(total_copies.values()):
+    for copy in pending + plane_copies + back_copies + score_copies + over_copies:
+        copy.wait_send()
+    for copy in total_copies.values():
         copy.wait_send()
     for group in y_copies:
         for copy in group:
             copy.wait_send()
 
 
-def per_device(out_grad, expert_ids, route_weights, down_weight, gate_pre, up_pre):
+def exchange(spare, out_grad, expert_ids, route_weights, down_weight, gate_pre, up_pre):
     tokens, width = out_grad.shape
     ff = down_weight.shape[1]
     rows = gate_pre.shape[1]
@@ -426,20 +463,21 @@
     wide = width + EXT
     vmem = pl.BlockSpec(memory_space=pltpu.VMEM)
     dma = pltpu.SemaphoreType.DMA
-    gate_out, up_out, route = pl.pallas_call(
-        kernel,
+    gate_out, up_out, route, over = pl.pallas_call(
+        functools.partial(kernel, spare),
         out_shape=(
             jax.ShapeDtypeStruct((ff, rows), BF16),
             jax.ShapeDtypeStruct((ff, rows), BF16),
             jax.ShapeDtypeStruct((2, tokens), F32),
+            jax.ShapeDtypeStruct((1, 1), jnp.int32),
         ),
         in_specs=[vmem, vmem, vmem, pl.BlockSpec(memory_space=pl.ANY), vmem, vmem],
-        out_specs=(vmem, vmem, vmem),
+        out_specs=(vmem, vmem, vmem, pl.BlockSpec(memory_space=pltpu.SMEM)),
         scratch_shapes=[
             pltpu.VMEM((256, wide), BF16),
             pltpu.VMEM((256, wide), BF16),
-            pltpu.VMEM((256, width // 2), BF16),
-            pltpu.VMEM((256, width // 2), BF16),
+            pltpu.VMEM((256, width // (16 // spare)), BF16),
+            pltpu.VMEM((256, width // (16 // spare)), BF16),
             pltpu.VMEM((2, 128, wide), BF16),
             pltpu.VMEM((2, 128, wide), BF16),
             pltpu.VMEM((128, width), BF16),
@@ -456,25 +494,37 @@
             pltpu.VMEM((PLANE, 8, 128), F32),
             pltpu.VMEM((8, 128), F32),
             pltpu.VMEM((ZN, 8, 128), F32),
-            dma((ZN, 4)), dma((ZN, 4)), dma((ZN,)), dma((ZN,)),
+            pltpu.VMEM((8, 128), F32),
+            pltpu.VMEM((SEQ, 8, 128), F32),
+            dma((ZN, 5)), dma((ZN, 5)), dma((ZN,)), dma((ZN,)),
             dma((6, PLANE)), dma((6, PLANE)), dma((3, SEQ)), dma((3, SEQ)),
             dma((3, SEQ)), dma((3, SEQ)), dma((PLANE,)), dma((PLANE,)),
-            dma((ZN,)), dma((ZN,)), dma,
+            dma((ZN,)), dma((ZN,)), dma((SEQ,)), dma((SEQ,)), dma,
         ],
         compiler_params=pltpu.CompilerParams(
-            collective_id=0, has_side_effects=True, vmem_limit_bytes=56 * 2**20
+            collective_id=0 if spare == 4 else 1, has_side_effects=True, vmem_limit_bytes=56 * 2**20
         ),
         cost_estimate=pl.CostEstimate(
             flops=2 * SEQ * ff * width * block, bytes_accessed=8 * 2**20, transcendentals=0
         ),
-        name="expert_backward",
+        name="expert_backward_%d" % spare,
     )(
         out_grad,
         expert_ids.T,
-        route_weights.T.astype(F32),
+        route_weights.T,
         down_weight[0],
         gate_pre[0].T,
         up_pre[0].T,
+    )
+    return gate_out, up_out, route, over
+
+
+def per_device(*arrays):
+    gate_out, up_out, route, over = exchange(4, *arrays)
+    gate_out, up_out, route = lax.cond(
+        over[0, 0] > 0,
+        lambda: exchange(8, *arrays)[:3],
+        lambda: (gate_out, up_out, route),
     )
     return gate_out.T[None], up_out.T[None], route.T
 

time: 197 us -> 173 us (0.88)
  Pallas kernels: 192 us -> 169 us
    pallas_call x1, Pallas kernels: 192 us -> 169 us  [exchange(): pl.pallas_call(functools.partial(kernel, spare), out_shape=(jax.ShapeDtyp...]
where the time goes in v3:
time: 173 us
  Pallas kernels  169 us (98%)
  local copies, waits for them, and re-layouts  2.22 us (1%)
    pallas_call x1, Pallas kernels, exchange(): pl.pallas_call(functools.partial(kernel, spare), out_shape=(jax.ShapeDtyp...  169 us

profile of v3, /device:TPU:1, one launch (start us, length us, event | category | flops | bytes accessed | tf_op | source)
XLA Modules:
  0.0 173.2 jit_solution(15236899782073268048)
XLA Ops:
  0.6 0.0 copy-start
  0.6 0.0 copy-start.1
  0.7 0.0 copy-start.2
  0.7 0.0 copy-start.3
  0.7 0.0 copy-start.4
  0.7 0.0 copy-start.5
  0.7 169.4 %expert_backward_4.1 = (bf16[192,1536]{1,0:T(8,128)(2,1)S(1)}, bf16[192,1536]{1,0:T(8,128)(2,1)S(1)}, f32[2,128]{1,0:T(2,128)S(1)}, s32[1,1]{1,0:T(1,128)}) custom-call(bf16[128,4096]{1,0:T(8,128)(2,1)} %x_ref.1, s32[2,128]{1,0:T(2,128)} %bitcast.35, bf16[2,128]{1,0:T(2,128)(2,1)} %bitcast.37, bf16[192,4096]{1,0:T(8,128)(2,1)} %bitcast.29, ...), custom_call_target="tpu_custom_call" | custom-call | flops 2415919104 | bytes 8388608 | tf_op jit(solution)/shard_map/expert_backward_4/pallas_call | solution.py:466
  170.7 0.0 copy-done
  170.7 0.0 copy-done.1
  170.7 0.0 copy-done.2
  170.8 0.0 copy-done.3
  170.8 0.0 copy-done.4
  170.8 0.0 copy-done.5
  170.8 0.2 conditional.1
  171.0 0.8 copy.18
  171.8 0.8 copy.19
  172.7 0.6 copy.20
Async XLA Ops:
  0.6 170.1 %copy-start = (bf16[1,192,4096]{2,1,0:T(8,128)(2,1)S(1)}, bf16[1,192,4096]{2,1,0:T(8,128)(2,1)}, u32[]{:S(2)}) copy-start(bf16[1,192,4096]{2,1,0:T(8,128)(2,1)} %param.11) | copy-start | bytes 4718596
  0.6 170.1 %copy-start.1 = (bf16[128,4096]{1,0:T(8,128)(2,1)S(1)}, bf16[128,4096]{1,0:T(8,128)(2,1)}, u32[]{:S(2)}) copy-start(bf16[128,4096]{1,0:T(8,128)(2,1)} %x_ref.1) | copy-start | bytes 3145732
  0.7 170.1 %copy-start.2 = (bf16[1,1536,192]{1,2,0:T(8,128)(2,1)S(1)}, bf16[1,1536,192]{1,2,0:T(8,128)(2,1)}, u32[]{:S(2)}) copy-start(bf16[1,1536,192]{1,2,0:T(8,128)(2,1)} %param.12) | copy-start | bytes 1769476
  0.7 170.1 %copy-start.3 = (bf16[1,1536,192]{1,2,0:T(8,128)(2,1)S(1)}, bf16[1,1536,192]{1,2,0:T(8,128)(2,1)}, u32[]{:S(2)}) copy-start(bf16[1,1536,192]{1,2,0:T(8,128)(2,1)} %param.13) | copy-start | bytes 1769476
  0.7 170.1 %copy-start.4 = (s32[128,2]{0,1:T(2,128)S(1)}, s32[128,2]{0,1:T(2,128)}, u32[]{:S(2)}) copy-start(s32[128,2]{0,1:T(2,128)} %param.9) | copy-start | bytes 3076
  0.7 170.1 %copy-start.5 = (bf16[128,2]{0,1:T(2,128)(2,1)S(1)}, bf16[128,2]{0,1:T(2,128)(2,1)}, u32[]{:S(2)}) copy-start(bf16[128,2]{0,1:T(2,128)(2,1)} %param.10) | copy-start | bytes 1540

commit v4 on v3

--- a/solution.py
+++ b/solution.py
@@ -9,7 +9,7 @@
 
 MESH = pl.DeviceIdType.MESH
 WINDOW = 8
-PIECES = 4
+PIECES = (1408, 1152, 1024, 512)
 SEQ, ZN, PLANE = 4, 16, 8
 SELF = 12
 EXT = 128
@@ -35,21 +35,20 @@
 
 
 def kernel(
-    spare, x_ref, ids_ref, rw_ref, w_ref, g_ref, u_ref,
+    spare, x_hbm, ids_ref, rw_ref, w_hbm, g_hbm, u_hbm,
     gg_ref, gu_ref, rg_ref, over_ref,
-    s_main, r_main, s_third, r_third, t_main, x_main, t_third, x_third,
-    w_all, g_all, u_all, g_perm, u_perm, acc, grads, back,
+    x_ref, g_ref, u_ref, s_main, r_main, s_third, r_third, t_main, x_main, t_third, x_third,
+    w_all, g_all, u_all, g_perm, u_perm, factors, restore, owner, acc, grads, back,
     score, score_in, total, total_in, over, over_in,
     z_s, z_r, zt_s, zt_r, p_s, p_r, y_s, y_r, b_s, b_r, ps_s, ps_r, zs_s, zs_r, o_s, o_r, local_sem,
 ):
     width = x_ref.shape[1]
-    ff = w_ref.shape[0]
+    ff = w_hbm.shape[0]
     block = g_ref.shape[1] // SEQ
     wide = width + EXT
     parts = 16 // spare
     span3 = width // parts
-    step = width // PIECES
-    pieces = [(EXT + step * n, step) for n in range(PIECES)]
+    pieces = [(EXT + sum(PIECES[:n]), size) for n, size in enumerate(PIECES)]
 
     s = lax.axis_index("seq")
     e = lax.axis_index("exp")
@@ -88,8 +87,14 @@
     for q in range(1, SEQ):
         pl.semaphore_signal(barrier, inc=1, device_id=y_from(q), device_id_type=MESH)
 
-    own_w = pltpu.make_async_copy(w_ref, w_all.at[pl.ds(0, ff)], local_sem)
-    own_w.start()
+    own = [
+        pltpu.make_async_copy(src, dst, local_sem.at[n])
+        for n, (src, dst) in enumerate(
+            ((x_hbm, x_ref), (w_hbm, w_all.at[pl.ds(0, ff)]), (g_hbm, g_ref), (u_hbm, u_ref))
+        )
+    ]
+    for copy in own:
+        copy.start()
 
     ids0, ids1 = ids_ref[0:1, :], ids_ref[1:2, :]
     w0, w1 = rw_ref[0:1, :].astype(F32), rw_ref[1:2, :].astype(F32)
@@ -131,7 +136,13 @@
     ).astype(BF16)
 
     score[...] = jnp.zeros((8, 128), F32)
-    own_w.wait()
+    own[0].wait()
+    for start in range(0, width, 1024):
+        s_main[128:256, EXT + start : EXT + start + 1024] = mm(
+            m_main[128:256], x_ref[:, start : start + 1024]
+        ).astype(BF16)
+    for copy in own[1:]:
+        copy.wait()
     pl.semaphore_wait(barrier, ZN - 1 + PLANE - 1 + SEQ - 1)
 
     y_copies = []
@@ -158,9 +169,10 @@
 
     whole = {k: main_copy(k, 0, wide, 0) for k in (8, 9, 15, 10, 14, 11, 13, 0)}
     part = {
-        (k, n): main_copy(k, start, size, n) for n, (start, size) in enumerate(pieces) for k in FAR
+        (k, n): main_copy(k, start if n else 0, size if n else EXT + size, n)
+        for n, (start, size) in enumerate(pieces)
+        for k in FAR
     }
-    extra = {k: main_copy(k, 0, EXT, PIECES) for k in FAR}
     third = {
         k: remote(
             s_third.at[pl.ds(16 * k, 16)], r_third.at[pl.ds(16 * k, 16)],
@@ -169,11 +181,7 @@
         for k in ALL_THIRD
     }
 
-    for start in range(0, width, 1024):
-        s_main[128:256, EXT + start : EXT + start + 1024] = mm(
-            m_main[128:256], x_ref[:, start : start + 1024]
-        ).astype(BF16)
-    for k in (8, 9, 15, 10):
+    for k in (8, 9, 15, 10, 14):
         issue(whole[k])
     for n in (0, 1, 2):
         for q in range(1, SEQ):
@@ -186,7 +194,7 @@
     for n in range(1, parts):
         packed_rows += mm(m_part[n], x_ref[:, span3 * n : span3 * n + span3])
     s_third[...] = packed_rows.astype(BF16)
-    for k in (14, 0, 11, 13):
+    for k in (0, 11, 13):
         issue(whole[k])
     r_main[16 * SELF : 16 * SELF + 16, :] = s_main[16 * SELF : 16 * SELF + 16, :]
     r_third[16 * SELF : 16 * SELF + 16, :] = s_third[16 * SELF : 16 * SELF + 16, :]
@@ -261,22 +269,50 @@
             g_perm[rows, :] = mm(g_all[rows, :], order).astype(BF16)
             u_perm[rows, :] = mm(u_all[rows, :], order).astype(BF16)
 
+    def orders():
+        restore[...] = hot(natural(iota((block, block), 0)) == iota((block, block), 1))
+        row = iota((128, 128), 0)
+        j = row >> 4
+        target = (((x + (j >> 1)) & 3) << 1) | ((c + (j & 1)) & 1)
+        for chunk in range(3):
+            if chunk == 1:
+                k, r = row & 15, jnp.full((128, 128), 2, jnp.int32)
+            else:
+                k, r = ((row >> 1) & 7) + (8 if chunk == 0 else 0), row & 1
+            expert = (((z - 4 - k) & 15) << 3) | target
+            first, second = ids0 == expert, ids1 == expert
+            match = mm(hot(first | second), earlier) == r.astype(F32)
+            owner[chunk, 0] = hot(first & match)
+            owner[chunk, 1] = hot(second & match)
+
+    def prepare(chunk):
+        lanes = slice(128 * chunk, 128 * chunk + 128)
+        for q in range(SEQ):
+            rows = slice(ff * q, ff * q + ff)
+            gate = g_perm[rows, lanes].astype(F32)
+            up = u_perm[rows, lanes].astype(F32)
+            sig = jax.nn.sigmoid(gate)
+            activated = gate * sig
+            factors[0, rows, :] = activated
+            factors[1, rows, :] = activated * up
+            factors[2, rows, :] = up * sig * (1.0 + gate * (1.0 - sig))
+
     back_copies = []
 
-    def finish(chunk, weights):
-        lanes = slice(128 * chunk, 128 * chunk + 128)
+    def finish(chunk, weights, cols=None):
         summed = jnp.zeros((1, 128), F32)
         for q in (2, 1, 3, 0):
             rows = slice(ff * q, ff * q + ff)
             projected = acc[rows, :]
-            gate = g_perm[rows, lanes].astype(F32)
-            up = u_perm[rows, lanes].astype(F32)
-            sig = jax.nn.sigmoid(gate)
-            activated = gate * sig
-            summed = summed + jnp.sum(activated * up * projected, axis=0, keepdims=True)
+            if cols is not None:
+                projected += mm_t(
+                    w_all[rows, cols[0] : cols[0] + cols[1]],
+                    x_main[1, :, EXT + cols[0] : EXT + cols[0] + cols[1]],
+                )
+            summed = summed + jnp.sum(factors[1, rows, :] * projected, axis=0, keepdims=True)
             scaled = weights * projected
-            grad_up = (scaled * activated).astype(BF16)
-            grad_gate = (scaled * up * sig * (1.0 + gate * (1.0 - sig))).astype(BF16)
+            grad_up = (scaled * factors[0, rows, :]).astype(BF16)
+            grad_gate = (scaled * factors[2, rows, :]).astype(BF16)
             if q:
                 grads[chunk, rows, 0:128] = grad_gate
                 grads[chunk, rows, 128:256] = grad_up
@@ -301,24 +337,44 @@
         match = match & (dst & 15 == ((src >> 1) & 7) + (8 if h == 0 else 0))
         return mm(weights.astype(BF16), hot(match))
 
-    for k in ALL_THIRD[:7]:
-        issue(extra[k])
-        issue(third[k])
+    for k in FAR[:4]:
+        issue(part[k, 0])
     for k in (8, 9, 15, 10, 14, 11, 13):
         whole[k].wait_recv()
     near_group = main_forward(0, 0, wide, 0)
-    for k in ALL_THIRD[7:]:
+    for k in FAR[4:]:
+        issue(part[k, 0])
+    for k in ALL_THIRD[:9]:
         issue(third[k])
     gates_ready()
-    for k in FAR:
-        issue(part[k, 0])
-    for k in FAR:
-        extra[k].wait_recv()
+    prepare(0)
+    far_groups = []
+
+    def far_forward(n):
+        for k in FAR:
+            part[k, n].wait_recv()
+        start, size = pieces[n]
+        if n == 0:
+            start, size = 0, EXT + size
+        far_groups.append(main_forward(1, start, size, 2 + n))
+
+    def far_product(n):
+        for copy in far_groups[n]:
+            copy.wait_recv()
+        start, size = pieces[n]
+        return mm_t(w_all[:, start - EXT : start - EXT + size], x_main[1, :, start : start + size])
+
+    for k in ALL_THIRD[9:]:
+        issue(third[k])
+    whole[0].wait_recv()
+    far_forward(0)
+    for k in FAR[:4]:
+        issue(part[k, 1])
+    orders()
     for k in ALL_THIRD:
         third[k].wait_recv()
-    whole[0].wait_recv()
     third_group = third_forward(1)
-    for k in FAR[:4]:
+    for k in FAR[4:]:
         issue(part[k, 1])
     for group in y_copies:
         group[2].wait_recv()
@@ -327,34 +383,17 @@
     acc[...] = mm_t(w_all[...], x_main[0, :, EXT:])
     near_weights = slot_weights(0)
     finish(0, near_weights[0:1, :])
-    far_groups = []
-
-    def far_forward(n):
-        for k in FAR:
-            part[k, n].wait_recv()
-        start, size = pieces[n]
-        if n == 0:
-            start, size = 0, EXT + size
-        far_groups.append(main_forward(1, start, size, 2 + n))
-
-    def far_product(n):
-        for copy in far_groups[n]:
-            copy.wait_recv()
-        product = mm_t(
-            w_all[:, step * n : step * n + step],
-            x_main[1, :, EXT + step * n : EXT + step * n + step],
-        )
-        if n == 0:
-            acc[...] = product
-        else:
-            acc[...] += product
-
-    far_forward(0)
+    for k in FAR[:4]:
+        issue(part[k, 2])
+    far_forward(1)
     for k in FAR[4:]:
-        issue(part[k, 1])
+        issue(part[k, 2])
     for copy in third_group:
         copy.wait_recv()
+    prepare(1)
     acc[...] = mm_t(w_all[...], x_third[...])
+    for k in FAR:
+        issue(part[k, 3])
     for copy in far_groups[0]:
         copy.wait_recv()
     far_weights = slot_weights(1)
@@ -369,22 +408,30 @@
         over_copies.append(copy)
     third_weights = spread(near_weights, 0) + spread(far_weights, 1)
     finish(1, third_weights[1:2, :])
-    for k in FAR[:4]:
-        issue(part[k, 2])
-    far_forward(1)
-    acc[...] = mm_t(w_all[:, 0:step], x_main[1, :, EXT : EXT + step])
-    for k in FAR[4:]:
-        issue(part[k, 2])
-    for k in FAR[:4]:
-        issue(part[k, 3])
+    prepare(2)
+    start, size = pieces[0]
+    acc[...] = mm_t(w_all[:, 0:size], x_main[1, :, start : start + size])
     far_forward(2)
-    far_product(1)
-    for k in FAR[4:]:
-        issue(part[k, 3])
-    far_product(2)
+    acc[...] += far_product(1)
+
+    def restored(q, chunks, first):
+        value = jnp.concatenate([back[n, q, :, first : first + 128] for n in chunks], axis=1)
+        return mm(value, restore[128 * chunks[0] : 128 * chunks[-1] + 128, :])
+
+    def home(q):
+        return pl.ds(pl.multiple_of(((s + q) & 3) * block, 128), block)
+
     far_forward(3)
-    far_product(3)
-    finish(2, far_weights[0:1, :])
+    for copy in back_copies:
+        copy.wait_recv()
+    early = len(back_copies)
+    for q in range(SEQ):
+        gg_ref[:, home(q)] = restored(q, (0, 1), 0).astype(BF16)
+        gu_ref[:, home(q)] = restored(q, (0, 1), 128).astype(BF16)
+    acc[...] += far_product(2)
+    for copy in far_groups[3]:
+        copy.wait_recv()
+    finish(2, far_weights[0:1, :], (pieces[3][0] - EXT, pieces[3][1]))
 
     score_copies = []
     for j in range(1, PLANE):
@@ -403,15 +450,11 @@
         copy.start()
         total_copies[k] = copy
 
-    restore = hot(natural(iota((block, block), 0)) == iota((block, block), 1))
-    for copy in back_copies:
+    for copy in back_copies[early:]:
         copy.wait_recv()
-    for q in range(SEQ):
-        lanes = pl.ds(pl.multiple_of(((s + q) & 3) * block, 128), block)
+    for q in (0, 1, 3, 2):
         for ref, first in ((gg_ref, 0), (gu_ref, 128)):
-            value = jnp.concatenate([back[n, q, :, first : first + 128] for n in range(3)], axis=1)
-            ref[:, lanes] = mm(value, restore).astype(BF16)
-
+            ref[:, home(q)] = (ref[:, home(q)].astype(F32) + restored(q, (2,), first)).astype(BF16)
     worst = over[...]
     for q in range(1, SEQ):
         over_copies[q - 1].wait_recv()
@@ -427,22 +470,12 @@
         total_copies[k].wait_recv()
         found = jnp.where(slot == k, total_in[k], found)
     columns = jnp.transpose(jnp.concatenate([found, jnp.zeros((120, 128), F32)], axis=0))
-    row = iota((128, 128), 0)
-    j = row >> 4
-    target = (((x + (j >> 1)) & 3) << 1) | ((c + (j & 1)) & 1)
     result0 = jnp.zeros((1, 128), F32)
     result1 = jnp.zeros((1, 128), F32)
     for chunk in range(3):
-        if chunk == 1:
-            k, r = row & 15, jnp.full((128, 128), 2, jnp.int32)
-        else:
-            k, r = ((row >> 1) & 7) + (8 if chunk == 0 else 0), row & 1
-        expert = (((z - 4 - k) & 15) << 3) | target
-        first, second = ids0 == expert, ids1 == expert
-        match = mm(hot(first | second), earlier) == r.astype(F32)
         column = columns[:, chunk : chunk + 1]
-        result0 += jnp.sum(jnp.where(first & match, column, 0.0), axis=0, keepdims=True)
-        result1 += jnp.sum(jnp.where(second & match, column, 0.0), axis=0, keepdims=True)
+        result0 += jnp.sum(jnp.where(owner[chunk, 0] > 0.5, column, 0.0), axis=0, keepdims=True)
+        result1 += jnp.sum(jnp.where(owner[chunk, 1] > 0.5, column, 0.0), axis=0, keepdims=True)
     rg_ref[0:1, :] = result0
     rg_ref[1:2, :] = result1
 
@@ -462,6 +495,7 @@
     block = rows // SEQ
     wide = width + EXT
     vmem = pl.BlockSpec(memory_space=pltpu.VMEM)
+    hbm = pl.BlockSpec(memory_space=pl.ANY)
     dma = pltpu.SemaphoreType.DMA
     gate_out, up_out, route, over = pl.pallas_call(
         functools.partial(kernel, spare),
@@ -471,9 +505,12 @@
             jax.ShapeDtypeStruct((2, tokens), F32),
             jax.ShapeDtypeStruct((1, 1), jnp.int32),
         ),
-        in_specs=[vmem, vmem, vmem, pl.BlockSpec(memory_space=pl.ANY), vmem, vmem],
+        in_specs=[hbm, vmem, vmem, hbm, hbm, hbm],
         out_specs=(vmem, vmem, vmem, pl.BlockSpec(memory_space=pltpu.SMEM)),
         scratch_shapes=[
+            pltpu.VMEM((tokens, width), BF16),
+            pltpu.VMEM((ff, rows), BF16),
+            pltpu.VMEM((ff, rows), BF16),
             pltpu.VMEM((256, wide), BF16),
             pltpu.VMEM((256, wide), BF16),
             pltpu.VMEM((256, width // (16 // spare)), BF16),
@@ -487,6 +524,9 @@
             pltpu.VMEM((SEQ * ff, block), BF16),
             pltpu.VMEM((SEQ * ff, block), BF16),
             pltpu.VMEM((SEQ * ff, block), BF16),
+            pltpu.VMEM((3, SEQ * ff, 128), F32),
+            pltpu.VMEM((block, block), BF16),
+            pltpu.VMEM((3, 2, 128, tokens), BF16),
             pltpu.VMEM((SEQ * ff, 128), F32),
             pltpu.VMEM((3, SEQ * ff, 256), BF16),
             pltpu.VMEM((3, SEQ, ff, 256), BF16),
@@ -496,10 +536,10 @@
             pltpu.VMEM((ZN, 8, 128), F32),
             pltpu.VMEM((8, 128), F32),
             pltpu.VMEM((SEQ, 8, 128), F32),
-            dma((ZN, 5)), dma((ZN, 5)), dma((ZN,)), dma((ZN,)),
+            dma((ZN, 4)), dma((ZN, 4)), dma((ZN,)), dma((ZN,)),
             dma((6, PLANE)), dma((6, PLANE)), dma((3, SEQ)), dma((3, SEQ)),
             dma((3, SEQ)), dma((3, SEQ)), dma((PLANE,)), dma((PLANE,)),
-            dma((ZN,)), dma((ZN,)), dma((SEQ,)), dma((SEQ,)), dma,
+            dma((ZN,)), dma((ZN,)), dma((SEQ,)), dma((SEQ,)), dma((4,)),
         ],
         compiler_params=pltpu.CompilerParams(
             collective_id=0 if spare == 4 else 1, has_side_effects=True, vmem_limit_bytes=56 * 2**20

time: 173 us -> 160 us (0.925)
  Pallas kernels: 169 us -> 156 us
    pallas_call x1, Pallas kernels: 169 us -> 156 us  [exchange(): pl.pallas_call(functools.partial(kernel, spare), out_shape=(jax.ShapeDtyp...]
where the time goes in v4:
time: 160 us
  Pallas kernels  156 us (98%)
  local copies, waits for them, and re-layouts  2.22 us (1%)
    pallas_call x1, Pallas kernels, exchange(): pl.pallas_call(functools.partial(kernel, spare), out_shape=(jax.ShapeDtyp...  156 us

profile of v4, /device:TPU:1, one launch (start us, length us, event | category | flops | bytes accessed | tf_op | source)
XLA Modules:
  0.0 159.7 jit_solution(14129054878152966606)
XLA Ops:
  0.6 0.0 copy-start
  0.6 0.0 copy-start.1
  0.7 0.0 copy-start.2
  0.7 0.0 copy-start.3
  0.7 0.0 copy-start.4
  0.7 0.0 copy-start.5
  0.7 155.9 %expert_backward_4.1 = (bf16[192,1536]{1,0:T(8,128)(2,1)S(1)}, bf16[192,1536]{1,0:T(8,128)(2,1)S(1)}, f32[2,128]{1,0:T(2,128)S(1)}, s32[1,1]{1,0:T(1,128)}) custom-call(bf16[128,4096]{1,0:T(8,128)(2,1)} %x_hbm.1, s32[2,128]{1,0:T(2,128)} %bitcast.35, bf16[2,128]{1,0:T(2,128)(2,1)} %bitcast.37, bf16[192,4096]{1,0:T(8,128)(2,1)} %bitcast.29, ...), custom_call_target="tpu_custom_call" | custom-call | flops 2415919104 | bytes 8388608 | tf_op jit(solution)/shard_map/expert_backward_4/pallas_call | solution.py:500
  157.3 0.0 copy-done
  157.3 0.0 copy-done.1
  157.3 0.0 copy-done.2
  157.3 0.0 copy-done.3
  157.3 0.0 copy-done.4
  157.3 0.0 copy-done.5
  157.3 0.2 conditional.1
  157.5 0.8 copy.18
  158.4 0.8 copy.19
  159.2 0.6 copy.20
Async XLA Ops:
  0.6 156.6 %copy-start = (bf16[1,192,4096]{2,1,0:T(8,128)(2,1)S(1)}, bf16[1,192,4096]{2,1,0:T(8,128)(2,1)}, u32[]{:S(2)}) copy-start(bf16[1,192,4096]{2,1,0:T(8,128)(2,1)} %param.11) | copy-start | bytes 4718596
  0.6 156.6 %copy-start.1 = (bf16[128,4096]{1,0:T(8,128)(2,1)S(1)}, bf16[128,4096]{1,0:T(8,128)(2,1)}, u32[]{:S(2)}) copy-start(bf16[128,4096]{1,0:T(8,128)(2,1)} %x_hbm.1) | copy-start | bytes 3145732
  0.7 156.6 %copy-start.2 = (bf16[1,1536,192]{1,2,0:T(8,128)(2,1)S(1)}, bf16[1,1536,192]{1,2,0:T(8,128)(2,1)}, u32[]{:S(2)}) copy-start(bf16[1,1536,192]{1,2,0:T(8,128)(2,1)} %param.12) | copy-start | bytes 1769476
  0.7 156.6 %copy-start.3 = (bf16[1,1536,192]{1,2,0:T(8,128)(2,1)S(1)}, bf16[1,1536,192]{1,2,0:T(8,128)(2,1)}, u32[]{:S(2)}) copy-start(bf16[1,1536,192]{1,2,0:T(8,128)(2,1)} %param.13) | copy-start | bytes 1769476
  0.7 156.6 %copy-start.4 = (s32[128,2]{0,1:T(2,128)S(1)}, s32[128,2]{0,1:T(2,128)}, u32[]{:S(2)}) copy-start(s32[128,2]{0,1:T(2,128)} %param.9) | copy-start | bytes 3076
  0.7 156.6 %copy-start.5 = (bf16[128,2]{0,1:T(2,128)(2,1)S(1)}, bf16[128,2]{0,1:T(2,128)(2,1)}, u32[]{:S(2)}) copy-start(bf16[128,2]{0,1:T(2,128)(2,1)} %param.10) | copy-start | bytes 1540

commit v5 on v4

--- a/solution.py
+++ b/solution.py
@@ -8,7 +8,7 @@
 from jax.sharding import PartitionSpec as P
 
 MESH = pl.DeviceIdType.MESH
-WINDOW = 8
+WINDOW = 14
 PIECES = (1408, 1152, 1024, 512)
 SEQ, ZN, PLANE = 4, 16, 8
 SELF = 12
@@ -45,10 +45,9 @@
     width = x_ref.shape[1]
     ff = w_hbm.shape[0]
     block = g_ref.shape[1] // SEQ
-    wide = width + EXT
     parts = 16 // spare
     span3 = width // parts
-    pieces = [(EXT + sum(PIECES[:n]), size) for n, size in enumerate(PIECES)]
+    pieces = [(sum(PIECES[:n]), size) for n, size in enumerate(PIECES)]
 
     s = lax.axis_index("seq")
     e = lax.axis_index("exp")
@@ -110,6 +109,69 @@
     is_main = named & (rank == upper.astype(F32))
     is_third = named & (rank == 2.0)
     m_main = hot(is_main)
+    score[...] = jnp.zeros((8, 128), F32)
+    own[0].wait()
+    for start in range(0, width, 1024):
+        s_main[128:256, start : start + 1024] = mm(
+            m_main[128:256], x_ref[:, start : start + 1024]
+        ).astype(BF16)
+    for copy in own[1:]:
+        copy.wait()
+    pl.semaphore_wait(barrier, ZN - 1 + PLANE - 1 + SEQ - 1)
+
+    y_copies = []
+    for q in range(1, SEQ):
+        rows = pl.ds(ff * q, ff)
+        lanes = pl.ds(pl.multiple_of(((s + q) & 3) * block, 128), block)
+        y_copies.append([
+            remote(g_ref.at[:, lanes], g_all.at[rows], y_s.at[0, q], y_r.at[0, q], y_to(q)),
+            remote(u_ref.at[:, lanes], u_all.at[rows], y_s.at[1, q], y_r.at[1, q], y_to(q)),
+            remote(w_all.at[pl.ds(0, ff)], w_all.at[rows], y_s.at[2, q], y_r.at[2, q], y_to(q)),
+        ])
+
+    pending, background = [], []
+
+    def issue(copy):
+        if len(pending) >= WINDOW:
+            pending.pop(0).wait_send()
+        copy.start()
+        pending.append(copy)
+        if background:
+            background.pop(0).start()
+
+    def flush():
+        while background:
+            background.pop(0).start()
+
+    def main_copy(k, start, size, n):
+        part = (pl.ds(16 * k, 16), pl.ds(start, size))
+        return remote(s_main.at[part], r_main.at[part], z_s.at[k, n], z_r.at[k, n], z_to(k))
+
+    whole = {k: main_copy(k, 0, width, 0) for k in (8, 9, 15, 10, 14, 11, 13, 0)}
+    part = {
+        (k, n): main_copy(k, start, size, n) for n, (start, size) in enumerate(pieces) for k in FAR
+    }
+    third = {
+        k: remote(
+            s_third.at[pl.ds(16 * k, 16)], r_third.at[pl.ds(16 * k, 16)],
+            zt_s.at[k], zt_r.at[k], z_to(k),
+        )
+        for k in ALL_THIRD
+    }
+
+    for k in (8, 9, 15, 10, 14, 11, 13):
+        issue(whole[k])
+    for n in (0, 1, 2):
+        for q in range(1, SEQ):
+            y_copies[q - 1][n].start()
+    for start in range(0, width, 1024):
+        s_main[0:128, start : start + 1024] = mm(
+            m_main[0:128], x_ref[:, start : start + 1024]
+        ).astype(BF16)
+    issue(whole[0])
+    for k in FAR[:3]:
+        issue(part[k, 0])
+
     m_third = hot(is_third)
     have = mm_t(jnp.ones((16, tokens), BF16), m_third)
     src, dst = iota((256, 256), 0), iota((256, 256), 1)
@@ -129,73 +191,16 @@
     value = jnp.where(named0, w0, w1)
     v_main = jnp.sum(jnp.where(is_main, value, 0.0), axis=1, keepdims=True)
     v_third = jnp.sum(jnp.where(is_third, value, 0.0), axis=1, keepdims=True)
-    s_main[:, 0:EXT] = jnp.where(
+    s_third[:, 0:EXT] = jnp.where(
         lane == 0,
         v_main,
         jnp.where(lane == 1, v_third, jnp.where(lane == 2, v_spot, jnp.where(lane == 3, excess, 0.0))),
     ).astype(BF16)
 
-    score[...] = jnp.zeros((8, 128), F32)
-    own[0].wait()
-    for start in range(0, width, 1024):
-        s_main[128:256, EXT + start : EXT + start + 1024] = mm(
-            m_main[128:256], x_ref[:, start : start + 1024]
-        ).astype(BF16)
-    for copy in own[1:]:
-        copy.wait()
-    pl.semaphore_wait(barrier, ZN - 1 + PLANE - 1 + SEQ - 1)
-
-    y_copies = []
-    for q in range(1, SEQ):
-        rows = pl.ds(ff * q, ff)
-        lanes = pl.ds(pl.multiple_of(((s + q) & 3) * block, 128), block)
-        y_copies.append([
-            remote(g_ref.at[:, lanes], g_all.at[rows], y_s.at[0, q], y_r.at[0, q], y_to(q)),
-            remote(u_ref.at[:, lanes], u_all.at[rows], y_s.at[1, q], y_r.at[1, q], y_to(q)),
-            remote(w_all.at[pl.ds(0, ff)], w_all.at[rows], y_s.at[2, q], y_r.at[2, q], y_to(q)),
-        ])
-
-    pending = []
-
-    def issue(copy):
-        if len(pending) >= WINDOW:
-            pending.pop(0).wait_send()
-        copy.start()
-        pending.append(copy)
-
-    def main_copy(k, start, size, n):
-        part = (pl.ds(16 * k, 16), pl.ds(start, size))
-        return remote(s_main.at[part], r_main.at[part], z_s.at[k, n], z_r.at[k, n], z_to(k))
-
-    whole = {k: main_copy(k, 0, wide, 0) for k in (8, 9, 15, 10, 14, 11, 13, 0)}
-    part = {
-        (k, n): main_copy(k, start if n else 0, size if n else EXT + size, n)
-        for n, (start, size) in enumerate(pieces)
-        for k in FAR
-    }
-    third = {
-        k: remote(
-            s_third.at[pl.ds(16 * k, 16)], r_third.at[pl.ds(16 * k, 16)],
-            zt_s.at[k], zt_r.at[k], z_to(k),
-        )
-        for k in ALL_THIRD
-    }
-
-    for k in (8, 9, 15, 10, 14):
-        issue(whole[k])
-    for n in (0, 1, 2):
-        for q in range(1, SEQ):
-            y_copies[q - 1][n].start()
-    for start in range(0, width, 1024):
-        s_main[0:128, EXT + start : EXT + start + 1024] = mm(
-            m_main[0:128], x_ref[:, start : start + 1024]
-        ).astype(BF16)
     packed_rows = mm(m_part[0], x_ref[:, 0:span3])
     for n in range(1, parts):
         packed_rows += mm(m_part[n], x_ref[:, span3 * n : span3 * n + span3])
-    s_third[...] = packed_rows.astype(BF16)
-    for k in (0, 11, 13):
-        issue(whole[k])
+    s_third[:, EXT:] = packed_rows.astype(BF16)
     r_main[16 * SELF : 16 * SELF + 16, :] = s_main[16 * SELF : 16 * SELF + 16, :]
     r_third[16 * SELF : 16 * SELF + 16, :] = s_third[16 * SELF : 16 * SELF + 16, :]
 
@@ -212,9 +217,9 @@
         for j in range(1, PLANE):
             area = (pl.ds(16 * j, 16), pl.ds(start, size))
             copy = remote(src.at[area], dst.at[area], p_s.at[n, j], p_r.at[n, j], p_to(j))
-            copy.start()
             group.append(copy)
         plane_copies.extend(group)
+        background.extend(group)
         dst[0:16, start : start + size] = src[0:16, start : start + size]
         return group
 
@@ -238,14 +243,17 @@
         column = iota((128, 256), 1)
         j = out_row >> 4
         p = (((x + (j >> 1)) & 3) << 1) | ((c + (j & 1)) & 1)
-        chosen = mm(hot(column == (out_row & 15) * 16 + p), r_main[:, 0:EXT])
+        chosen = mm(hot(column == (out_row & 15) * 16 + p), r_third[:, 0:EXT])
         spot = chosen[:, 2:3] - 1.0
         spot = (out_row & 15 == column >> 4) & (spot == (column & (spare - 1)).astype(F32))
         part_of = (column & 15) >> (spare.bit_length() - 1)
         for m in range(parts):
             match = hot(spot & (part_of == m))
-            t_third[:, span3 * m : span3 * m + span3] = mm(match, r_third[...]).astype(BF16)
-        return plane_send(t_third, x_third, 0, width, n)
+            at = 2 * EXT + span3 * m
+            t_third[:, at : at + span3] = mm(match, r_third[:, EXT:]).astype(BF16)
+        t_third[:, 0:EXT] = mm(regroup, r_third[128:256, 0:EXT]).astype(BF16)
+        t_third[:, EXT : 2 * EXT] = mm(regroup, r_third[0:128, 0:EXT]).astype(BF16)
+        return plane_send(t_third, x_third, 0, 2 * EXT + width, n)
 
     def natural(index):
         chunk, low = index >> 7, index & 127
@@ -298,6 +306,14 @@
             factors[2, rows, :] = up * sig * (1.0 + gate * (1.0 - sig))
 
     back_copies = []
+    score_copies = []
+
+    def send_scores():
+        for j in range(1, PLANE):
+            copy = remote(score, score_in.at[j], ps_s.at[j], ps_r.at[j], p_from(j))
+            copy.start()
+            score_copies.append(copy)
+
 
     def finish(chunk, weights, cols=None):
         summed = jnp.zeros((1, 128), F32)
@@ -307,9 +323,16 @@
             if cols is not None:
                 projected += mm_t(
                     w_all[rows, cols[0] : cols[0] + cols[1]],
-                    x_main[1, :, EXT + cols[0] : EXT + cols[0] + cols[1]],
+                    x_main[1, :, cols[0] : cols[0] + cols[1]],
                 )
+                acc[rows, :] = projected
             summed = summed + jnp.sum(factors[1, rows, :] * projected, axis=0, keepdims=True)
+        score[chunk : chunk + 1, :] = summed
+        if cols is not None:
+            send_scores()
+        for q in (2, 1, 3, 0):
+            rows = slice(ff * q, ff * q + ff)
+            projected = acc[rows, :]
             scaled = weights * projected
             grad_up = (scaled * factors[0, rows, :]).astype(BF16)
             grad_gate = (scaled * factors[2, rows, :]).astype(BF16)
@@ -325,11 +348,10 @@
             else:
                 back[chunk, 0, :, 0:128] = grad_gate
                 back[chunk, 0, :, 128:256] = grad_up
-        score[chunk : chunk + 1, :] = summed
 
     def slot_weights(h):
         pick = hot(iota((16, 128), 0) == iota((16, 128), 1))
-        return mm_t(pick, x_main[h, :, 0:EXT])
+        return mm_t(pick, x_third[:, EXT * h : EXT * h + EXT])
 
     def spread(weights, h):
         src, dst = iota((128, 128), 0), iota((128, 128), 1)
@@ -337,12 +359,10 @@
         match = match & (dst & 15 == ((src >> 1) & 7) + (8 if h == 0 else 0))
         return mm(weights.astype(BF16), hot(match))
 
-    for k in FAR[:4]:
-        issue(part[k, 0])
     for k in (8, 9, 15, 10, 14, 11, 13):
         whole[k].wait_recv()
-    near_group = main_forward(0, 0, wide, 0)
-    for k in FAR[4:]:
+    near_group = main_forward(0, 0, width, 0)
+    for k in FAR[3:]:
         issue(part[k, 0])
     for k in ALL_THIRD[:9]:
         issue(third[k])
@@ -353,16 +373,15 @@
     def far_forward(n):
         for k in FAR:
             part[k, n].wait_recv()
-        start, size = pieces[n]
-        if n == 0:
-            start, size = 0, EXT + size
-        far_groups.append(main_forward(1, start, size, 2 + n))
+        far_groups.append(main_forward(1, pieces[n][0], pieces[n][1], 2 + n))
+        if n > 1:
+            flush()
 
     def far_product(n):
         for copy in far_groups[n]:
             copy.wait_recv()
         start, size = pieces[n]
-        return mm_t(w_all[:, start - EXT : start - EXT + size], x_main[1, :, start : start + size])
+        return mm_t(w_all[:, start : start + size], x_main[1, :, start : start + size])
 
     for k in ALL_THIRD[9:]:
         issue(third[k])
@@ -376,28 +395,24 @@
     third_group = third_forward(1)
     for k in FAR[4:]:
         issue(part[k, 1])
-    for group in y_copies:
-        group[2].wait_recv()
-    for copy in near_group:
-        copy.wait_recv()
-    acc[...] = mm_t(w_all[...], x_main[0, :, EXT:])
-    near_weights = slot_weights(0)
-    finish(0, near_weights[0:1, :])
     for k in FAR[:4]:
         issue(part[k, 2])
     far_forward(1)
     for k in FAR[4:]:
         issue(part[k, 2])
+    for k in FAR:
+        issue(part[k, 3])
+    flush()
+    for group in y_copies:
+        group[2].wait_recv()
+    for copy in near_group:
+        copy.wait_recv()
+    acc[...] = mm_t(w_all[...], x_main[0])
     for copy in third_group:
         copy.wait_recv()
-    prepare(1)
-    acc[...] = mm_t(w_all[...], x_third[...])
-    for k in FAR:
-        issue(part[k, 3])
-    for copy in far_groups[0]:
-        copy.wait_recv()
-    far_weights = slot_weights(1)
-    seen = jnp.maximum(x_main[0, :, 0:EXT].astype(F32), x_main[1, :, 0:EXT].astype(F32))
+    near_weights, far_weights = slot_weights(0), slot_weights(1)
+    finish(0, near_weights[0:1, :])
+    seen = jnp.maximum(x_third[:, 0:EXT].astype(F32), x_third[:, EXT : 2 * EXT].astype(F32))
     seen = jnp.max(seen, axis=0, keepdims=True)
     seen = jnp.max(jnp.where(iota((1, 128), 1) == 3, seen, 0.0), axis=1, keepdims=True)
     over[...] = jnp.broadcast_to(seen, (8, 128))
@@ -406,11 +421,12 @@
         copy = remote(over, over_in.at[q], o_s.at[q], o_r.at[q], y_to(q))
         copy.start()
         over_copies.append(copy)
+    prepare(1)
+    acc[...] = mm_t(w_all[...], x_third[:, 2 * EXT :])
     third_weights = spread(near_weights, 0) + spread(far_weights, 1)
     finish(1, third_weights[1:2, :])
     prepare(2)
-    start, size = pieces[0]
-    acc[...] = mm_t(w_all[:, 0:size], x_main[1, :, start : start + size])
+    acc[...] = far_product(0)
     far_forward(2)
     acc[...] += far_product(1)
 
@@ -431,13 +447,8 @@
     acc[...] += far_product(2)
     for copy in far_groups[3]:
         copy.wait_recv()
-    finish(2, far_weights[0:1, :], (pieces[3][0] - EXT, pieces[3][1]))
-
-    score_copies = []
-    for j in range(1, PLANE):
-        copy = remote(score, score_in.at[j], ps_s.at[j], ps_r.at[j], p_from(j))
-        copy.start()
-        score_copies.append(copy)
+    finish(2, far_weights[0:1, :], pieces[3])
+
     place = iota((8, 128), 1)
     gathered = jnp.where(place >> 4 == 0, score[...], 0.0)
     for j in range(1, PLANE):
@@ -493,7 +504,7 @@
     ff = down_weight.shape[1]
     rows = gate_pre.shape[1]
     block = rows // SEQ
-    wide = width + EXT
+    third = width // (16 // spare)
     vmem = pl.BlockSpec(memory_space=pltpu.VMEM)
     hbm = pl.BlockSpec(memory_space=pl.ANY)
     dma = pltpu.SemaphoreType.DMA
@@ -511,14 +522,14 @@
             pltpu.VMEM((tokens, width), BF16),
             pltpu.VMEM((ff, rows), BF16),
             pltpu.VMEM((ff, rows), BF16),
-            pltpu.VMEM((256, wide), BF16),
-            pltpu.VMEM((256, wide), BF16),
-            pltpu.VMEM((256, width // (16 // spare)), BF16),
-            pltpu.VMEM((256, width // (16 // spare)), BF16),
-            pltpu.VMEM((2, 128, wide), BF16),
-            pltpu.VMEM((2, 128, wide), BF16),
-            pltpu.VMEM((128, width), BF16),
-            pltpu.VMEM((128, width), BF16),
+            pltpu.VMEM((256, width), BF16),
+            pltpu.VMEM((256, width), BF16),
+            pltpu.VMEM((256, EXT + third), BF16),
+            pltpu.VMEM((256, EXT + third), BF16),
+            pltpu.VMEM((2, 128, width), BF16),
+            pltpu.VMEM((2, 128, width), BF16),
+            pltpu.VMEM((128, 2 * EXT + width), BF16),
+            pltpu.VMEM((128, 2 * EXT + width), BF16),
             pltpu.VMEM((SEQ * ff, width), BF16),
             pltpu.VMEM((SEQ * ff, block), BF16),
             pltpu.VMEM((SEQ * ff, block), BF16),

time: 160 us -> 159 us (level)
  no operation moved by 1% of the time
where the time goes in v5:
time: 159 us
  Pallas kernels  155 us (97%)
  local copies, waits for them, and re-layouts  2.22 us (1%)
    pallas_call x1, Pallas kernels, exchange(): pl.pallas_call(functools.partial(kernel, spare), out_shape=(jax.ShapeDtyp...  155 us

profile of v5, /device:TPU:1, one launch (start us, length us, event | category | flops | bytes accessed | tf_op | source)
XLA Modules:
  0.0 158.7 jit_solution(16502208994888948309)
XLA Ops:
  0.6 0.0 copy-start
  0.6 0.0 copy-start.1
  0.7 0.0 copy-start.2
  0.7 0.0 copy-start.3
  0.7 0.0 copy-start.4
  0.7 0.0 copy-start.5
  0.7 154.9 %expert_backward_4.1 = (bf16[192,1536]{1,0:T(8,128)(2,1)S(1)}, bf16[192,1536]{1,0:T(8,128)(2,1)S(1)}, f32[2,128]{1,0:T(2,128)S(1)}, s32[1,1]{1,0:T(1,128)}) custom-call(bf16[128,4096]{1,0:T(8,128)(2,1)} %x_hbm.1, s32[2,128]{1,0:T(2,128)} %bitcast.35, bf16[2,128]{1,0:T(2,128)(2,1)} %bitcast.37, bf16[192,4096]{1,0:T(8,128)(2,1)} %bitcast.29, ...), custom_call_target="tpu_custom_call" | custom-call | flops 2415919104 | bytes 8388608 | tf_op jit(solution)/shard_map/expert_backward_4/pallas_call | solution.py:511
  156.2 0.0 copy-done
  156.2 0.0 copy-done.1
  156.2 0.0 copy-done.2
  156.2 0.0 copy-done.3
  156.2 0.0 copy-done.4
  156.3 0.0 copy-done.5
  156.3 0.2 conditional.1
  156.5 0.8 copy.18
  157.3 0.8 copy.19
  158.1 0.6 copy.20
Async XLA Ops:
  0.6 155.6 %copy-start = (bf16[1,192,4096]{2,1,0:T(8,128)(2,1)S(1)}, bf16[1,192,4096]{2,1,0:T(8,128)(2,1)}, u32[]{:S(2)}) copy-start(bf16[1,192,4096]{2,1,0:T(8,128)(2,1)} %param.11) | copy-start | bytes 4718596
  0.6 155.6 %copy-start.1 = (bf16[128,4096]{1,0:T(8,128)(2,1)S(1)}, bf16[128,4096]{1,0:T(8,128)(2,1)}, u32[]{:S(2)}) copy-start(bf16[128,4096]{1,0:T(8,128)(2,1)} %x_hbm.1) | copy-start | bytes 3145732
  0.7 155.6 %copy-start.2 = (bf16[1,1536,192]{1,2,0:T(8,128)(2,1)S(1)}, bf16[1,1536,192]{1,2,0:T(8,128)(2,1)}, u32[]{:S(2)}) copy-start(bf16[1,1536,192]{1,2,0:T(8,128)(2,1)} %param.12) | copy-start | bytes 1769476
  0.7 155.6 %copy-start.3 = (bf16[1,1536,192]{1,2,0:T(8,128)(2,1)S(1)}, bf16[1,1536,192]{1,2,0:T(8,128)(2,1)}, u32[]{:S(2)}) copy-start(bf16[1,1536,192]{1,2,0:T(8,128)(2,1)} %param.13) | copy-start | bytes 1769476
  0.7 155.6 %copy-start.4 = (s32[128,2]{0,1:T(2,128)S(1)}, s32[128,2]{0,1:T(2,128)}, u32[]{:S(2)}) copy-start(s32[128,2]{0,1:T(2,128)} %param.9) | copy-start | bytes 3076
  0.7 155.6 %copy-start.5 = (bf16[128,2]{0,1:T(2,128)(2,1)S(1)}, bf16[128,2]{0,1:T(2,128)(2,1)}, u32[]{:S(2)}) copy-start(bf16[128,2]{0,1:T(2,128)(2,1)} %param.10) | copy-start | bytes 1540
